TPU v7x, 256 devices: a whole 4x4x8 slice. The times are simulated.
256 devices in a mesh: blk: 64 (over z, y_hi, x), col: 4 (over y_lo, core).
Axes of the slice: x: 4, y: 4 (y_hi: 2, y_lo: 2; y = y_hi * 2 + y_lo), z: 8, core: 2. Of those that a mesh axis runs over, the one named last changes fastest.
Arguments:
- points: float32 [16, 65536], P(None, 'blk'), may hold values from -5 to 5
- lengths: float32 [16], replicated, may hold values from 2 to 4
- noise: float32 [65536], P('blk'), may hold values from 0.5 to 2
- outscale: float32 [1], replicated, may hold values from 0.02 to 0.1
- solution: float32 [32, 65536], P('col', 'blk'), may hold values from -6 to 6
- residual: float32 [32, 65536], P('col', 'blk'), may hold values from -26 to 26
- direction: float32 [32, 65536], P('col', 'blk'), may hold values from -31 to 31
Outputs:
- solution_next: float32 [32, 65536], P('col', 'blk')
- residual_next: float32 [32, 65536], P('col', 'blk')
- direction_next: float32 [32, 65536], P('col', 'blk')
All inputs are finite; a program needn't handle non-finite values.
Results may differ from a plain program's by a relative error of at most 0.0003.
Values may be sent and summed in bfloat16 or wider, within the bound.
No kernel may reach another device: no remote copies, remote signals or barrier semaphores. Data moves between devices by JAX's collectives and lax.ppermute only.
A program may use at most 64 MiB of HBM per device.

v0:
```python
import math

import jax
import jax.numpy as jnp
from jax import lax
from jax.sharding import PartitionSpec as P


def matern_tile(left, right, amplitude):
    cross = lax.dot_general(
        left,
        right,
        (((0,), (0,)), ((), ())),
        precision=lax.Precision.HIGHEST,
        preferred_element_type=jnp.float32,
    )
    left_sq = jnp.sum(left * left, axis=0)
    right_sq = jnp.sum(right * right, axis=0)
    dist_sq = jnp.maximum(left_sq[:, None] + right_sq[None, :] - 2.0 * cross, 0.0)
    radius = jnp.sqrt(5.0 * dist_sq)
    return (amplitude * (1.0 + radius + radius * radius / 3.0) * jnp.exp(-radius)).astype(
        jnp.bfloat16
    )


def local(points, lengths, noise, outscale, solution, residual, direction):
    amplitude = outscale[0]
    scaled = points / lengths[:, None]
    local_count = scaled.shape[1]
    lowered = direction.astype(jnp.bfloat16)
    norm_now = lax.psum(jnp.sum(residual * residual, axis=1), "blk")
    columns = lax.all_gather(lowered, "col", axis=0, tiled=True)
    row_count = local_count // lax.axis_size("col")
    offset_rows = lax.axis_index("col") * row_count
    rows_points = lax.dynamic_slice_in_dim(scaled, offset_rows, row_count, 1)
    column_count = columns.shape[0]
    every_columns = lax.all_gather(columns, "blk", axis=1, tiled=True)
    initial = jnp.zeros((column_count, row_count), jnp.float32)
    piece_points = lax.all_gather(scaled.astype(jnp.bfloat16), "blk", axis=1, tiled=True).astype(
        jnp.float32
    )
    block_width = math.gcd(piece_points.shape[1], 4096)
    block_count = piece_points.shape[1] // block_width

    def block_step(index_block, running):
        some_points = lax.dynamic_slice_in_dim(
            piece_points, index_block * block_width, block_width, 1
        )
        some_columns = lax.dynamic_slice_in_dim(
            every_columns, index_block * block_width, block_width, 1
        )
        kernel_tile = matern_tile(some_points, rows_points, amplitude)
        return running + jnp.dot(some_columns, kernel_tile, preferred_element_type=jnp.float32)

    direct = lax.fori_loop(0, block_count, block_step, initial)
    kernel_image = lax.all_to_all(direct, "col", split_axis=0, concat_axis=1, tiled=True)
    image = kernel_image + noise[None, :] * direction
    curve = lax.psum(jnp.sum(direction * image, axis=1), "blk")
    alpha = norm_now / curve
    solution_next = solution + alpha[:, None] * direction
    residual_next = residual - alpha[:, None] * image
    norm_next = lax.psum(jnp.sum(residual_next * residual_next, axis=1), "blk")
    direction_next = residual_next + (norm_next / norm_now)[:, None] * direction
    return (solution_next, residual_next, direction_next)


def solution(mesh):
    in_specs = (
        P(None, "blk"),
        P(),
        P("blk"),
        P(),
        P("col", "blk"),
        P("col", "blk"),
        P("col", "blk"),
    )
    out_specs = (P("col", "blk"), P("col", "blk"), P("col", "blk"))
    return jax.shard_map(local, mesh=mesh, in_specs=in_specs, out_specs=out_specs, check_vma=False)
```

profile of v0, /device:TPU:8, one launch (start us, length us, event | category | flops | bytes accessed | tf_op | source)
XLA Modules:
  0.0 807.8 jit_solution(12915426682235332588)
XLA Ops:
  7.2 1.5 fusion.8
  8.8 0.0 all-gather.3.cloned.1.call-start
  8.8 0.8 convert_element_type.18
  9.6 5.8 all_gather.9
  15.5 116.2 %all-gather.5.cloned.1.call-done = bf16[16,65536]{1,0:T(8,128)(2,1)} async-done(((bf16[16,1024]{1,0:T(8,128)(2,1)}), bf16[16,65536]{1,0:T(8,128)(2,1)}) %all-gather.5.cloned.1.call-update) | async-done | bytes 2097168 | tf_op jit(solution)/shard_map/all_gather | solution.py:39
  131.6 3.8 convert_element_type.20
  135.5 124.2 %all-gather.3.cloned.1.call-done = bf16[32,65536]{1,0:T(8,128)(2,1)} async-done(((bf16[32,1024]{1,0:T(8,128)(2,1)}), bf16[32,65536]{1,0:T(8,128)(2,1)}) %all-gather.3.cloned.1.call-update) | async-done | bytes 4194320 | tf_op jit(solution)/shard_map/all_gather | solution.py:37
  259.7 177.2 %while.16 = (s32[]{:T(128)}, f32[32,256]{1,0:T(8,128)}, bf16[32,65536]{1,0:T(8,128)(2,1)}, f32[]{:T(128)}, f32[16,65536]{1,0:T(8,128)}, /*index=5*/f32[256]{0:T(...) while((s32[]{:T(128)}, f32[32,256]{1,0:T(8,128)}, ...), condition=%wide.region_5.0_spmd.clone, body=%wide.region_3.5_spmd.clone.sunk | while | flops 282210304 | bytes 5097137 | solution.py:55
  259.7 1.0 multiply_reduce_fusion.6
  260.7 8.0 multiply_convert_fusion.2
  268.7 2.0 convolution_add_fusion.2
  270.8 1.0 multiply_reduce_fusion.6
  271.8 8.0 multiply_convert_fusion.2
  279.8 2.0 convolution_add_fusion.2
  281.9 1.0 multiply_reduce_fusion.6
  282.9 8.0 multiply_convert_fusion.2
  290.9 2.0 convolution_add_fusion.2
  292.9 1.0 multiply_reduce_fusion.6
  293.9 8.0 multiply_convert_fusion.2
  302.0 2.0 convolution_add_fusion.2
  304.0 1.0 multiply_reduce_fusion.6
  305.0 8.0 multiply_convert_fusion.2
  313.0 2.0 convolution_add_fusion.2
  315.1 1.0 multiply_reduce_fusion.6
  316.1 8.0 multiply_convert_fusion.2
  324.1 2.0 convolution_add_fusion.2
  326.1 1.0 multiply_reduce_fusion.6
  327.1 8.0 multiply_convert_fusion.2
  335.2 2.0 convolution_add_fusion.2
  337.2 1.0 multiply_reduce_fusion.6
  338.2 8.0 multiply_convert_fusion.2
  346.2 2.0 convolution_add_fusion.2
  348.3 1.0 multiply_reduce_fusion.6
  349.3 8.0 multiply_convert_fusion.2
  357.3 2.0 convolution_add_fusion.2
  359.4 1.0 multiply_reduce_fusion.6
  360.4 8.0 multiply_convert_fusion.2
  368.4 2.0 convolution_add_fusion.2
  370.4 1.0 multiply_reduce_fusion.6
  371.4 8.0 multiply_convert_fusion.2
  379.5 2.0 convolution_add_fusion.2
  381.5 1.0 multiply_reduce_fusion.6
  382.5 8.0 multiply_convert_fusion.2
  390.5 2.0 convolution_add_fusion.2
  392.6 1.0 multiply_reduce_fusion.6
  393.6 8.0 multiply_convert_fusion.2
  401.6 2.0 convolution_add_fusion.2
  403.6 1.0 multiply_reduce_fusion.6
  404.6 8.0 multiply_convert_fusion.2
  412.7 2.0 convolution_add_fusion.2
  414.7 1.0 multiply_reduce_fusion.6
  415.7 8.0 multiply_convert_fusion.2
  423.7 2.0 convolution_add_fusion.2
  425.8 1.0 multiply_reduce_fusion.6
  426.8 8.0 multiply_convert_fusion.2
  434.8 2.0 convolution_add_fusion.2
  436.9 4.7 all-to-all-start
  441.5 0.1 multiply_reduce_fusion.3
  441.7 1.8 all-to-all-done
  443.5 0.1 multiply_reduce_fusion.2
  443.6 179.4 %all-reduce = (f32[8]{0:T(128)S(1)}, f32[8]{0:T(128)S(1)}) all-reduce(f32[8]{0:T(128)S(1)} %multiply_reduce_fusion.3, f32[8]{0:T(128)S(1)} %multiply_reduce_fusion.2), channel_id=1, replica_groups=mesh['blk'=64,'col'=4] {'blk'}, use_global_device_ids=true, to_apply=%region_1.0 | all-reduce | flops 16 | bytes 128 | tf_op jit(solution)/shard_map/psum | solution.py:31
  623.1 0.8 multiply_reduce_fusion.1
  623.9 176.4 %psum.23 = f32[8]{0:T(128)S(1)} all-reduce(f32[8]{0:T(128)S(1)} %get-tuple-element.198), channel_id=1, replica_groups=mesh['blk'=64,'col'=4] {'blk'}, use_global_device_ids=true, to_apply=%region_9.0 | all-reduce | flops 8 | bytes 64 | tf_op jit(solution)/shard_map/psum | solution.py:62
  800.3 0.7 multiply_add_fusion
  (17 shorter events, 0.1 us)
Async XLA Ops:
  7.2 124.5 %all-gather.5.cloned.1.call-start = ((), (), s32[]{:S(2)}) async-start(), calls=%async_computation.2 | async-start | bytes 2129920 | tf_op jit(solution)/shard_map/all_gather | solution.py:39
  8.8 250.9 %all-gather.3.cloned.1.call-start = ((), (), s32[]{:S(2)}) async-start(), calls=%async_computation.1 | async-start | bytes 4259840 | tf_op jit(solution)/shard_map/all_gather | solution.py:37
  259.7 181.9 %copy-start.2 = (f32[8,1024]{1,0:T(8,128)S(1)}, f32[8,1024]{1,0:T(8,128)}, u32[]{:S(2)}) copy-start(f32[8,1024]{1,0:T(8,128)} %param.14) | copy-start | bytes 98308
  259.7 183.8 %copy-start = (f32[8,1024]{1,0:T(8,128)S(1)}, f32[8,1024]{1,0:T(8,128)}, u32[]{:S(2)}) copy-start(f32[8,1024]{1,0:T(8,128)} %param.15) | copy-start | bytes 98308
  259.7 183.8 %copy-start.4 = (f32[1024]{0:T(1024)S(1)}, f32[1024]{0:T(1024)}, u32[]{:S(2)}) copy-start(f32[1024]{0:T(1024)} %param.11) | copy-start | bytes 12292
  259.7 363.4 %copy-start.3 = (f32[8,1024]{1,0:T(8,128)S(1)}, f32[8,1024]{1,0:T(8,128)}, u32[]{:S(2)}) copy-start(f32[8,1024]{1,0:T(8,128)} %param.13) | copy-start | bytes 98308
  436.9 6.6 all-to-all-start
  623.9 177.1 %copy-start.1 = (f32[8,1024]{1,0:T(8,128)}, f32[8,1024]{1,0:T(8,128)S(1)}, u32[]{:S(2)}) copy-start(f32[8,1024]{1,0:T(8,128)S(1)} %get-tuple-element.199) | copy-start | bytes 98308
Sparse Core Ops, SparseCore 0:
  12.1 119.5 all-gather.4
  135.2 124.4 all-gather.2
where the time goes:
time: 812 us; the launch traced here: 808 us
  blocking collectives  362 us (45%)
  waiting for transfers between devices  242 us (30%)
  matrix products  161 us (20%)
  other arithmetic  23.9 us (3%)
  between operations  14.1 us (2%)
    psum x1, blocking collectives, local(): norm_now = lax.psum(jnp.sum(residual * residual, axis=1), 'blk')  179 us
    psum x1, blocking collectives, local(): norm_next = lax.psum(jnp.sum(residual_next * residual_next, axis=1), 'blk')  176 us
    dot_general x16, matrix products, matern_tile(): lax.dot_general(left, right, (((0,), (0,)), ((), ())), precision=lax.Prec...  128 us
    all_gather x1, waiting for transfers between devices, local(): every_columns = lax.all_gather(columns, 'blk', axis=1, tiled=True)  124 us
    all_gather x1, waiting for transfers between devices, local(): lax.all_gather(scaled.astype(jnp.bfloat16), 'blk', axis=1, tiled=True)  116 us
    dot_general x16, matrix products, block_step(): jnp.dot(some_columns, kernel_tile, preferred_element_type=jnp.float32)  32.7 us
  transfers between devices with their start and end apart: 3, of which 3 were waited for; matrix products, arithmetic and copies ran while one was open for 1% of the time, Pallas kernels for 0%

commit v1 on v0

v1 whole, which is shorter than its diff:
```python
import functools
import math

import jax
import jax.numpy as jnp
from jax import lax
from jax.experimental import pallas as pl
from jax.experimental.pallas import tpu as pltpu
from jax.sharding import Mesh, PartitionSpec as P

F32 = jnp.float32
BF16 = jnp.bfloat16
KAPPA = 1.0 / math.log(2.0)
SHIFT = -1.5 * KAPPA
CONST = 0.75 * KAPPA * KAPPA
FACTOR = math.exp(1.5) / (3.0 * KAPPA * KAPPA)
TINY = 1e-30

BLK = ("z", "yh", "x")
COL = ("yl", "core")
NEAR = ("x", "yl", "core")
FAR = ("z", "yh")


def split3(value):
    high = value.astype(BF16).astype(F32)
    rest = value - high
    middle = rest.astype(BF16).astype(F32)
    return high, middle, rest - middle


def matern(dist):
    dist = jnp.maximum(dist, TINY)
    t = SHIFT - dist * lax.rsqrt(dist)
    return ((t * t + CONST) * jnp.exp2(t)).astype(BF16)


def stack_rows(rows, width):
    index = lax.broadcasted_iota(jnp.int32, (16, width), 0)
    total = jnp.zeros((16, width), F32)
    for place, row in enumerate(rows):
        total = jnp.where(index == place, row, total)
    return total


def image_kernel(tile_i, tile_j, rows_ref, cols_ref, out_ref, row_f, col_f, low, dist_s, kern_s):
    groups, _, width = rows_ref.shape
    pieces, _, piece = cols_ref.shape
    count_i = groups * width
    count_j = pieces * piece

    def row_features(g, _):
        value = rows_ref[g]
        norm = split3(jnp.sum(value * value, axis=0, keepdims=True))
        one = jnp.ones((1, width), F32)
        misc = stack_rows((*norm, one, one, one), width)
        parts = jnp.concatenate([*split3(value), misc], axis=0)
        row_f[:, pl.ds(pl.multiple_of(g * width, width), width)] = parts.astype(BF16)
        return 0

    lax.fori_loop(0, groups, row_features, 0)

    def col_features(p, _):
        value = cols_ref[p, 32:48, :].astype(F32)
        norm = split3(jnp.sum(value * value, axis=0, keepdims=True))
        one = jnp.ones((1, piece), F32)
        misc = stack_rows((one, one, one, *norm), piece)
        cross = -2.0 * value
        parts = jnp.concatenate([cross, cross, cross, misc], axis=0)
        place = pl.ds(pl.multiple_of(p * piece, piece), piece)
        col_f[place, :] = parts.T.astype(BF16)
        low[:, place] = cols_ref[p, 0:32, :]
        return 0

    lax.fori_loop(0, pieces, col_features, 0)

    per = count_j // tile_j
    steps = (count_i // tile_i) * per
    per_group = width // tile_i

    def spot_i(step):
        return pl.ds(pl.multiple_of((step // per) * tile_i, tile_i), tile_i)

    def spot_j(step):
        return pl.ds(pl.multiple_of((step % per) * tile_j, tile_j), tile_j)

    def distances(step, slot):
        dist_s[slot] = jnp.dot(
            col_f[spot_j(step), :], row_f[:, spot_i(step)], preferred_element_type=F32
        )

    def accumulate(step, slot):
        tile = step // per
        group = tile // per_group
        place = pl.ds(pl.multiple_of((tile % per_group) * tile_i, tile_i), tile_i)
        out_ref[group, :, place] += jnp.dot(
            low[:, spot_j(step)], kern_s[slot], preferred_element_type=F32
        )

    out_ref[...] = jnp.zeros_like(out_ref)
    kern_s[1] = jnp.zeros((tile_j, tile_i), BF16)
    distances(0, 0)

    def one(step, slot):
        accumulate(jnp.maximum(step - 1, 0), 1 - slot)
        distances(jnp.minimum(step + 1, steps - 1), 1 - slot)
        for a in range(0, tile_j, 16):
            kern_s[slot, a : a + 16, :] = matern(dist_s[slot, a : a + 16, :])

    def two(pair, _):
        one(2 * pair, 0)
        one(2 * pair + 1, 1)
        return 0

    lax.fori_loop(0, steps // 2, two, 0)
    accumulate(steps - 1, 1)


def kernel_image(rows, cols, tile_i=256, tile_j=512):
    groups, _, width = rows.shape
    pieces, _, piece = cols.shape
    count_i, count_j = groups * width, pieces * piece
    vmem = pl.BlockSpec(memory_space=pltpu.VMEM)
    return pl.pallas_call(
        functools.partial(image_kernel, tile_i, tile_j),
        out_shape=jax.ShapeDtypeStruct((groups, 32, width), F32),
        in_specs=[vmem, vmem],
        out_specs=vmem,
        scratch_shapes=[
            pltpu.VMEM((64, count_i), BF16),
            pltpu.VMEM((count_j, 64), BF16),
            pltpu.VMEM((32, count_j), BF16),
            pltpu.VMEM((2, tile_j, tile_i), F32),
            pltpu.VMEM((2, tile_j, tile_i), BF16),
        ],
        compiler_params=pltpu.CompilerParams(vmem_limit_bytes=40 * 2**20),
        cost_estimate=pl.CostEstimate(
            flops=2 * count_i * count_j * 96,
            bytes_accessed=4 * 1024 * 1024,
            transcendentals=2 * count_i * count_j,
        ),
        name="kernel_image",
    )(rows, cols)


def spread(value, axes, count):
    return lax.all_to_all(
        jnp.broadcast_to(value[None], (count, *value.shape)), axes, 0, 0, tiled=True
    )


def local(points, lengths, noise, outscale, solution, residual, direction):
    far = lax.axis_size(FAR)
    near = lax.axis_size(NEAR)
    cols = lax.axis_size(COL)
    own, count = direction.shape
    piece = count // cols

    scaled = points * ((KAPPA * math.sqrt(5.0)) / lengths)[:, None]
    lowered = direction.astype(BF16)
    columns = lax.all_to_all(lowered, COL, 1, 0, tiled=True)
    some = lax.dynamic_slice_in_dim(scaled, lax.axis_index(COL) * piece, piece, 1)
    packet = jnp.concatenate([columns, some.astype(BF16)], axis=0)
    packets = spread(packet, FAR, far)
    rows = spread(scaled, "x", lax.axis_size("x"))

    partial = kernel_image(rows, packets)
    partial = lax.all_to_all(partial.reshape(near, own, count), NEAR, 0, 0, tiled=True)
    image = (FACTOR * outscale[0]) * jnp.sum(partial, axis=0) + noise[None, :] * direction

    sums = jnp.concatenate(
        [
            jnp.sum(residual * residual, axis=1),
            jnp.sum(direction * image, axis=1),
            jnp.sum(residual * image, axis=1),
            jnp.sum(image * image, axis=1),
        ]
    )
    sums = jnp.sum(spread(sums, BLK, lax.axis_size(BLK)), axis=0).reshape(4, own)
    norm_now, curve, mixed, square = sums[0], sums[1], sums[2], sums[3]
    alpha = norm_now / curve
    norm_next = jnp.maximum(norm_now - alpha * (2.0 * mixed - alpha * square), 0.0)
    solution_next = solution + alpha[:, None] * direction
    residual_next = residual - alpha[:, None] * image
    direction_next = residual_next + (norm_next / norm_now)[:, None] * direction
    return (solution_next, residual_next, direction_next)


def solution(mesh):
    fine = Mesh(mesh.devices.reshape(8, 2, 4, 2, 2), (*BLK, *COL))
    in_specs = (
        P(None, BLK),
        P(),
        P(BLK),
        P(),
        P(COL, BLK),
        P(COL, BLK),
        P(COL, BLK),
    )
    out_specs = (P(COL, BLK), P(COL, BLK), P(COL, BLK))
    return jax.shard_map(local, mesh=fine, in_specs=in_specs, out_specs=out_specs, check_vma=False)
```

time: 812 us -> 108 us (0.13)
  blocking collectives: 362 us -> 40.3 us
  waiting for transfers between devices: 242 us -> 17.4 us
  matrix products: 161 us -> 0 us
  Pallas kernels: 0 us -> 29.3 us
  other arithmetic: 23.9 us -> 2.63 us
  between operations: 14.1 us -> 1.38 us
  starting transfers between devices: 4.75 us -> 15 us
    psum x2 -> x0, blocking collectives: 356 us -> none  [the longest x1 179 us: local(): norm_now = lax.psum(jnp.sum(residual * residual, axis=1), 'blk')]
    all_gather x2 -> x0, waiting for transfers between devices: 240 us -> none  [the longest x1 124 us: local(): every_columns = lax.all_gather(columns, 'blk', axis=1, tiled=True)]
    dot_general x32 -> x0, matrix products: 161 us -> none  [the longest x16 128 us: matern_tile(): lax.dot_general(left, right, (((0,), (0,)), ((), ())), precision=lax.Prec...]
    all_to_all x0 -> x2, blocking collectives: none -> 40.3 us  [spread(): lax.all_to_all(jnp.broadcast_to(value[None], (count, *value.shape)), axes...]
    pallas_call x0 -> x1, Pallas kernels: none -> 29.3 us  [kernel_image(): pl.pallas_call(functools.partial(image_kernel, tile_i, tile_j), out_shape...]
    reduce_sum x20 -> x3, other arithmetic: 17.1 us -> 0.28 us  [the longest x1 0.16 us: local(): jnp.sum(residual * residual, axis=1)]
    all_to_all x1 -> x3, waiting for transfers between devices: 1.82 us -> 17.4 us  [the longest x1 8.67 us: local(): lax.all_to_all(partial.reshape(near, own, count), NEAR, 0, 0, tiled=True)]
    all_to_all x1 -> x3, starting transfers between devices: 4.67 us -> 15 us  [the longest x1 6.01 us: local(): lax.all_to_all(partial.reshape(near, own, count), NEAR, 0, 0, tiled=True)]
  transfers between devices with their start and end apart: 3 -> 3, of which waited for: 3 -> 3; matrix products, arithmetic and copies ran while one was open for 1% -> 0% of each run, Pallas kernels for 0% -> 0%
where the time goes in v1:
time: 108 us; the launch traced here: 107 us
  blocking collectives  40.3 us (37%)
  Pallas kernels  29.3 us (27%)
  waiting for transfers between devices  17.4 us (16%)
  starting transfers between devices  15 us (14%)
  other arithmetic  2.63 us (2%)
  local copies, waits for them, and re-layouts  1.39 us (1%)
  between operations  1.38 us (1%)
    all_to_all x2, blocking collectives, spread(): lax.all_to_all(jnp.broadcast_to(value[None], (count, *value.shape)), axes...  40.3 us
    pallas_call x1, Pallas kernels, kernel_image(): pl.pallas_call(functools.partial(image_kernel, tile_i, tile_j), out_shape...  29.3 us
    all_to_all x1, waiting for transfers between devices, local(): lax.all_to_all(partial.reshape(near, own, count), NEAR, 0, 0, tiled=True)  8.67 us
    all_to_all x1, waiting for transfers between devices, spread(): lax.all_to_all(jnp.broadcast_to(value[None], (count, *value.shape)), axes...  6.91 us
    all_to_all x1, starting transfers between devices, local(): lax.all_to_all(partial.reshape(near, own, count), NEAR, 0, 0, tiled=True)  6.01 us
    all_to_all x1, starting transfers between devices, local(): columns = lax.all_to_all(lowered, COL, 1, 0, tiled=True)  5.54 us
    all_to_all x1, starting transfers between devices, spread(): lax.all_to_all(jnp.broadcast_to(value[None], (count, *value.shape)), axes...  3.4 us
  transfers between devices with their start and end apart: 3, of which 3 were waited for; matrix products, arithmetic and copies ran while one was open for 0% of the time, Pallas kernels for 0%

profile of v1, /device:TPU:8, one launch (start us, length us, event | category | flops | bytes accessed | tf_op | source)
XLA Modules:
  0.0 107.3 jit_solution(17984281634553488093)
XLA Ops:
  0.6 0.0 copy-start.2
  0.6 1.4 %convert_element_type.6 = bf16[8,1024]{1,0:T(8,128)(2,1)} convert(f32[8,1024]{1,0:T(8,128)} %param.13) | non-fusion elementwise | flops 8192 | bytes 49152 | tf_op jit(solution)/shard_map/convert_element_type | solution.py:160
  2.0 0.0 copy-start.5
  2.0 5.5 %all-to-all-start.1 = ((bf16[8,4,256]{2,0,1:T(8,128)(2,1)}), bf16[8,4,256]{2,0,1:T(8,128)(2,1)S(1)}, u32[]{:S(2)}, u32[]{:S(2)}) async-start(bf16[8,4,256]{2,0,1:T(8,128)(2,1)} %bitcast.1), calls=%async_computation.1 | async-start | bytes 32768 | tf_op jit(solution)/shard_map/all_to_all | solution.py:161
  7.6 0.0 copy-done.5
  7.6 0.0 copy-done.2
  7.6 0.1 broadcast_multiply_fusion
  7.7 1.8 %all-to-all-done.1 = bf16[8,4,256]{2,0,1:T(8,128)(2,1)S(1)} async-done(((bf16[8,4,256]{2,0,1:T(8,128)(2,1)}), bf16[8,4,256]{2,0,1:T(8,128)(2,1)S(1)}, u32[]{:S(2)}, u32[]{:S(2)}) %all-to-all-start.1) | async-done | bytes 16416 | tf_op jit(solution)/shard_map/all_to_all | solution.py:161
  9.4 0.7 broadcast_in_dim.6
  10.2 3.4 %all-to-all-start = ((f32[4,16,1024]{2,1,0:T(8,128)}), f32[4,16,1024]{2,1,0:T(8,128)S(1)}, u32[]{:S(2)}, u32[]{:S(2)}) async-start(f32[4,16,1024]{2,1,0:T(8,128)} %broadcast_in_dim.6), calls=%async_computation | async-start | bytes 524288 | tf_op jit(solution)/shard_map/all_to_all | solution.py:147
  13.6 6.9 %all-to-all-done.rows_ref = f32[4,16,1024]{2,1,0:T(8,128)S(1)} async-done(((f32[4,16,1024]{2,1,0:T(8,128)}), f32[4,16,1024]{2,1,0:T(8,128)S(1)}, u32[]{:S(2)}, u32[]{:S(2)}) %all-to-all-start) | async-done | bytes 262176 | tf_op jit(solution)/shard_map/all_to_all | solution.py:147
  20.5 24.1 %all_to_all.40.cols_ref = bf16[16,48,256]{2,1,0:T(8,128)(2,1)S(1)} all-to-all(bf16[16,48,256]{2,1,0:T(8,128)(2,1)S(1)} %broadcast_in_dim.7), channel_id=1, replica_groups=mesh['z'=8,'yh'=2,'x'=4,'yl'=2,'core'=2] {'z','yh'}, dimensions={0} | all-to-all | bytes 786432 | tf_op jit(solution)/shard_map/all_to_all | solution.py:147
  44.6 29.3 %kernel_image.1 = f32[4,32,1024]{2,1,0:T(8,128)} custom-call(f32[4,16,1024]{2,1,0:T(8,128)S(1)} %all-to-all-done.rows_ref, bf16[16,48,256]{2,1,0:T(8,128)(2,1)S(1)} %all_to_all.40.cols_ref), custom_call_target="tpu_custom_call" | custom-call | flops 3221225472 | bytes 4194304 | tf_op jit(solution)/shard_map/kernel_image/pallas_call | solution.py:124
  73.9 0.0 copy-start.4
  73.9 6.0 %all-to-all-start.3 = ((f32[16,8,1024]{2,1,0:T(8,128)}), f32[16,8,1024]{2,1,0:T(8,128)S(1)}, u32[]{:S(2)}, u32[]{:S(2)}) async-start(f32[16,8,1024]{2,1,0:T(8,128)} %bitcast.4), calls=%async_computation.3 | async-start | bytes 1048576 | tf_op jit(solution)/shard_map/all_to_all | solution.py:168
  80.6 0.0 copy-start
  80.6 0.0 copy-start.1
  80.6 8.7 %all-to-all-done.3 = f32[16,8,1024]{2,1,0:T(8,128)S(1)} async-done(((f32[16,8,1024]{2,1,0:T(8,128)}), f32[16,8,1024]{2,1,0:T(8,128)S(1)}, u32[]{:S(2)}, u32[]{:S(2)}) %all-to-all-start.3) | async-done | bytes 524320 | tf_op jit(solution)/shard_map/all_to_all | solution.py:168
  89.3 0.0 copy-done.4
  89.3 0.0 copy-done
  89.3 0.0 copy-done.1
  89.3 0.2 multiply_reduce_fusion.3
  89.5 0.1 pad_maximum_fusion.1
  89.6 16.2 %all_to_all.41 = f32[64,1,32]{2,1,0:T(1,128)S(1)} all-to-all(f32[64,1,32]{2,1,0:T(1,128)S(1)} %broadcast_in_dim.8), channel_id=1, replica_groups=mesh['z'=8,'yh'=2,'x'=4,'yl'=2,'core'=2] {'z','yh','x'}, dimensions={0} | all-to-all | bytes 16384 | tf_op jit(solution)/shard_map/all_to_all | solution.py:147
  105.8 0.0 copy-start.3
  105.8 0.1 reduce_sum.59
  105.9 0.1 maximum_divide_fusion
  106.0 0.6 copy-done.3
  106.5 0.7 multiply_add_fusion
  (6 shorter events, 0.1 us)
Async XLA Ops:
  0.6 7.0 %copy-start.2 = (f32[16,1024]{1,0:T(8,128)S(1)}, f32[16,1024]{1,0:T(8,128)}, u32[]{:S(2)}) copy-start(f32[16,1024]{1,0:T(8,128)} %param.7) | copy-start | bytes 196612
  2.0 5.5 %copy-start.5 = (f32[16]{0:T(128)S(1)}, f32[16]{0:T(128)}, u32[]{:S(2)}) copy-start(f32[16]{0:T(128)} %param.8) | copy-start | bytes 196
  2.0 7.4 %all-to-all-start.1 = ((bf16[8,4,256]{2,0,1:T(8,128)(2,1)}), bf16[8,4,256]{2,0,1:T(8,128)(2,1)S(1)}, u32[]{:S(2)}, u32[]{:S(2)}) async-start(bf16[8,4,256]{2,0,1:T(8,128)(2,1)} %bitcast.1), calls=%async_computation.1 | async-start | bytes 32768 | tf_op jit(solution)/shard_map/all_to_all | solution.py:161
  10.2 10.4 %all-to-all-start = ((f32[4,16,1024]{2,1,0:T(8,128)}), f32[4,16,1024]{2,1,0:T(8,128)S(1)}, u32[]{:S(2)}, u32[]{:S(2)}) async-start(f32[4,16,1024]{2,1,0:T(8,128)} %broadcast_in_dim.6), calls=%async_computation | async-start | bytes 524288 | tf_op jit(solution)/shard_map/all_to_all | solution.py:147
  73.9 15.4 %copy-start.4 = (f32[1024]{0:T(1024)S(1)}, f32[1024]{0:T(1024)}, u32[]{:S(2)}) copy-start(f32[1024]{0:T(1024)} %param.9) | copy-start | bytes 12292
  73.9 15.4 %all-to-all-start.3 = ((f32[16,8,1024]{2,1,0:T(8,128)}), f32[16,8,1024]{2,1,0:T(8,128)S(1)}, u32[]{:S(2)}, u32[]{:S(2)}) async-start(f32[16,8,1024]{2,1,0:T(8,128)} %bitcast.4), calls=%async_computation.3 | async-start | bytes 1048576 | tf_op jit(solution)/shard_map/all_to_all | solution.py:168
  80.6 8.7 %copy-start = (f32[8,1024]{1,0:T(8,128)S(1)}, f32[8,1024]{1,0:T(8,128)}, u32[]{:S(2)}) copy-start(f32[8,1024]{1,0:T(8,128)} %param.13) | copy-start | bytes 98308
  80.6 8.7 %copy-start.1 = (f32[8,1024]{1,0:T(8,128)S(1)}, f32[8,1024]{1,0:T(8,128)}, u32[]{:S(2)}) copy-start(f32[8,1024]{1,0:T(8,128)} %param.12) | copy-start | bytes 98308
  105.8 0.8 copy-start.3

commit v2 on v1

v2 whole, which is shorter than its diff:
```python
import functools
import math

import jax
import jax.numpy as jnp
from jax import lax
from jax.experimental import pallas as pl
from jax.experimental.pallas import tpu as pltpu
from jax.sharding import Mesh, PartitionSpec as P

F32 = jnp.float32
BF16 = jnp.bfloat16
KAPPA = 1.0 / math.log(2.0)
SHIFT = -1.5 * KAPPA
CONST = 0.75 * KAPPA * KAPPA
FACTOR = math.exp(1.5) / (3.0 * KAPPA * KAPPA)
TINY = 1e-30

BLK = ("z", "yh", "x")
COL = ("yl", "core")
NEAR = ("x", "yl", "core")
FAR = ("z", "yh")


def split3(value):
    high = value.astype(BF16).astype(F32)
    rest = value - high
    middle = rest.astype(BF16).astype(F32)
    return high, middle, rest - middle


def stack_rows(rows, width):
    index = lax.broadcasted_iota(jnp.int32, (16, width), 0)
    total = jnp.zeros((16, width), F32)
    for place, row in enumerate(rows):
        total = jnp.where(index == place, row, total)
    return total


def row_kernel(x_ref, own_ref, *refs):
    others, out_ref = refs[:-1], refs[-1]
    width = own_ref.shape[1]
    groups = len(others) + 1
    for step, ref in enumerate((own_ref, *others)):
        value = ref[...]
        norm = split3(jnp.sum(value * value, axis=0, keepdims=True))
        one = jnp.ones((1, width), F32)
        misc = stack_rows((*norm, one, one, one), width)
        parts = jnp.concatenate([*split3(value), misc], axis=0)
        group = lax.rem(x_ref[0] + step, groups)
        out_ref[:, pl.ds(pl.multiple_of(group * width, width), width)] = parts.astype(BF16)


def row_features(index, blocks):
    count = sum(block.shape[1] for block in blocks)
    vmem = pl.BlockSpec(memory_space=pltpu.VMEM)
    return pl.pallas_call(
        row_kernel,
        out_shape=jax.ShapeDtypeStruct((64, count), BF16),
        in_specs=[pl.BlockSpec(memory_space=pltpu.SMEM)] + [vmem] * len(blocks),
        out_specs=vmem,
        name="row_features",
    )(index, *blocks)


def image_kernel(tile_i, tile_j, core_ref, rows_ref, packets_ref, keep_ref, send_ref, *scratch):
    col_f, low, dist_s, expo_s, kern_s = scratch
    pieces = packets_ref.shape[0] // 4
    piece = 256
    half = piece // 2
    count_i = rows_ref.shape[1]
    count_j = pieces * piece
    width = keep_ref.shape[2]
    core = core_ref[0]

    def col_features(p, _):
        parts = [packets_ref[4 * p + q].astype(F32) for q in range(4)]
        value = jnp.concatenate(
            [
                jnp.concatenate([parts[0][:, piece:], parts[1][:, piece:]], axis=1),
                jnp.concatenate([parts[2][:, piece:], parts[3][:, piece:]], axis=1),
            ],
            axis=0,
        )
        norm = split3(jnp.sum(value * value, axis=0, keepdims=True))
        one = jnp.ones((1, piece), F32)
        misc = stack_rows((one, one, one, *norm), piece)
        cross = -2.0 * value
        place = pl.ds(pl.multiple_of(p * piece, piece), piece)
        col_f[place, :] = jnp.concatenate([cross, cross, cross, misc], axis=0).T.astype(BF16)
        mine = [packets_ref[4 * p + core].astype(F32), packets_ref[4 * p + 2 + core].astype(F32)]
        rest = [packets_ref[4 * p + 1 - core].astype(F32), packets_ref[4 * p + 3 - core].astype(F32)]
        columns = jnp.concatenate([part[:, :piece] for part in mine + rest], axis=0)
        low[:, place] = columns.astype(BF16)
        return 0

    lax.fori_loop(0, pieces, col_features, 0)

    per = count_j // tile_j
    steps = (count_i // tile_i) * per
    per_group = width // tile_i

    def spot_i(step):
        return pl.ds(pl.multiple_of((step // per) * tile_i, tile_i), tile_i)

    def spot_j(step):
        return pl.ds(pl.multiple_of((step % per) * tile_j, tile_j), tile_j)

    def distances(step, slot):
        dist_s[slot] = jnp.dot(
            col_f[spot_j(step), :], rows_ref[:, spot_i(step)], preferred_element_type=F32
        )

    def exponents(slot, a):
        dist = jnp.maximum(dist_s[slot, a : a + 16, :], TINY)
        expo_s[slot, a : a + 16, :] = SHIFT - dist * lax.rsqrt(dist)

    def entries(slot, a):
        t = expo_s[slot, a : a + 16, :]
        kern_s[slot, a : a + 16, :] = ((t * t + CONST) * jnp.exp2(t)).astype(BF16)

    def accumulate(step, slot):
        tile = step // per
        group = tile // per_group
        place = pl.ds(pl.multiple_of((tile % per_group) * tile_i, tile_i), tile_i)
        product = jnp.dot(low[:, spot_j(step)], kern_s[slot], preferred_element_type=F32)
        keep_ref[group, :, place] += product[:16]
        send_ref[group, :, place] += product[16:]

    keep_ref[...] = jnp.zeros_like(keep_ref)
    send_ref[...] = jnp.zeros_like(send_ref)
    kern_s[1] = jnp.zeros((tile_j, tile_i), BF16)
    distances(0, 0)
    distances(1, 1)
    for a in range(0, tile_j, 16):
        exponents(0, a)

    def one(step, slot):
        accumulate(jnp.maximum(step - 1, 0), 1 - slot)
        for a in range(0, tile_j, 16):
            entries(slot, a)
            exponents(1 - slot, a)
        distances(jnp.minimum(step + 2, steps - 1), slot)

    def four(index, _):
        for k in range(4):
            one(4 * index + k, k % 2)
        return 0

    lax.fori_loop(0, steps // 4, four, 0)
    accumulate(steps - 1, 1)


def kernel_image(core, rows, packets, width, tile_i=256, tile_j=1024):
    count_i, count_j = rows.shape[1], packets.shape[0] // 4 * 256
    vmem = pl.BlockSpec(memory_space=pltpu.VMEM)
    shape = jax.ShapeDtypeStruct((count_i // width, 16, width), F32)
    return pl.pallas_call(
        functools.partial(image_kernel, tile_i, tile_j),
        out_shape=(shape, shape),
        in_specs=[pl.BlockSpec(memory_space=pltpu.SMEM), vmem, vmem],
        out_specs=(vmem, vmem),
        scratch_shapes=[
            pltpu.VMEM((count_j, 64), BF16),
            pltpu.VMEM((32, count_j), BF16),
            pltpu.VMEM((2, tile_j, tile_i), F32),
            pltpu.VMEM((2, tile_j, tile_i), F32),
            pltpu.VMEM((2, tile_j, tile_i), BF16),
        ],
        compiler_params=pltpu.CompilerParams(vmem_limit_bytes=40 * 2**20),
        cost_estimate=pl.CostEstimate(
            flops=2 * count_i * count_j * 96,
            bytes_accessed=4 * 1024 * 1024,
            transcendentals=2 * count_i * count_j,
        ),
        name="kernel_image",
    )(core, rows, packets)


def spread(value, axes, count):
    return lax.all_to_all(
        jnp.broadcast_to(value[None], (count, *value.shape)), axes, 0, 0, tiled=True
    )


def local(points, lengths, noise, outscale, solution, residual, direction):
    far, near, line = lax.axis_size(FAR), lax.axis_size(NEAR), lax.axis_size("x")
    cols = lax.axis_size(COL)
    own, count = direction.shape
    piece = count // cols
    yl, core = lax.axis_index("yl"), lax.axis_index("core")

    scaled = points * ((KAPPA * math.sqrt(5.0)) / lengths)[:, None]
    blocks = [scaled] + [
        lax.ppermute(scaled, "x", [(i, (i - step) % line) for i in range(line)])
        for step in range(1, line)
    ]
    rows = row_features(lax.axis_index("x")[None], blocks)

    lowered = direction.astype(BF16).reshape(own, cols, piece)
    part = lax.dynamic_slice_in_dim(scaled, yl * 8, 8, 0).reshape(8, cols, piece)
    part = lax.dynamic_slice_in_dim(part, core * (piece // 2), piece // 2, 2).astype(BF16)
    packet = jnp.concatenate([lowered, part], axis=2).transpose(1, 0, 2)
    packets = jnp.broadcast_to(packet[None], (far, *packet.shape))
    packets = packets.reshape(far * cols, *packet.shape[1:])
    packets = lax.all_to_all(packets, FAR + COL, 0, 0, tiled=True)

    keep, send = kernel_image(core[None], rows, packets, count)
    keep = keep + lax.ppermute(send, "core", [(0, 1), (1, 0)])
    partial = keep.reshape(near // 2, own, count)
    partial = lax.all_to_all(partial, ("x", "yl"), 0, 0, tiled=True)
    image = (FACTOR * outscale[0]) * jnp.sum(partial, axis=0) + noise[None, :] * direction

    sums = jnp.concatenate(
        [
            jnp.sum(residual * residual, axis=1),
            jnp.sum(direction * image, axis=1),
            jnp.sum(residual * image, axis=1),
            jnp.sum(image * image, axis=1),
        ]
    )
    sums = spread(sums, BLK, lax.axis_size(BLK))
    sums = jnp.sum(sums, axis=0).reshape(4, own)
    norm_now, curve, mixed, square = sums[0], sums[1], sums[2], sums[3]
    alpha = norm_now / curve
    norm_next = jnp.maximum(norm_now - alpha * (2.0 * mixed - alpha * square), 0.0)
    solution_next = solution + alpha[:, None] * direction
    residual_next = residual - alpha[:, None] * image
    direction_next = residual_next + (norm_next / norm_now)[:, None] * direction
    return (solution_next, residual_next, direction_next)


def solution(mesh):
    fine = Mesh(mesh.devices.reshape(8, 2, 4, 2, 2), (*BLK, *COL))
    in_specs = (
        P(None, BLK),
        P(),
        P(BLK),
        P(),
        P(COL, BLK),
        P(COL, BLK),
        P(COL, BLK),
    )
    out_specs = (P(COL, BLK), P(COL, BLK), P(COL, BLK))
    return jax.shard_map(local, mesh=fine, in_specs=in_specs, out_specs=out_specs, check_vma=False)
```

time: 108 us -> 89.8 us (0.83)
  blocking collectives: 40.3 us -> 17.7 us
  starting transfers between devices: 15 us -> 22.8 us
  Pallas kernels: 29.3 us -> 25.7 us
  waiting for transfers between devices: 17.4 us -> 14.8 us
  local copies, waits for them, and re-layouts: 1.39 us -> 3.1 us
    all_to_all x2 -> x1, blocking collectives: 40.3 us -> 17.7 us  [spread(): lax.all_to_all(jnp.broadcast_to(value[None], (count, *value.shape)), axes...]
    all_to_all x3 -> x2, waiting for transfers between devices: 17.4 us -> 8.42 us  [the longest x1 5.79 us: local(): partial = lax.all_to_all(partial, ('x', 'yl'), 0, 0, tiled=True)]
    ppermute x0 -> x4, waiting for transfers between devices: none -> 6.42 us  [the longest x3 5.08 us: local(): lax.ppermute(scaled, 'x', [(i, (i - step) % line) for i in range(line)])]
    pallas_call x1, Pallas kernels: 29.3 us -> 23.8 us  [kernel_image(): pl.pallas_call(functools.partial(image_kernel, tile_i, tile_j), out_shape...]
    ppermute x0 -> x4, starting transfers between devices: none -> 4.81 us  [the longest x3 4.52 us: local(): lax.ppermute(scaled, 'x', [(i, (i - step) % line) for i in range(line)])]
    all_to_all x3 -> x2, starting transfers between devices: 15 us -> 18 us  [the longest x1 12.1 us: local(): packets = lax.all_to_all(packets, FAR + COL, 0, 0, tiled=True)]
    pallas_call x0 -> x1, Pallas kernels: none -> 1.88 us  [row_features(): pl.pallas_call(row_kernel, out_shape=jax.ShapeDtypeStruct((64, count), BF...]
    unnamed x12 -> x20, local copies, waits for them, and re-layouts: 0.61 us -> 2.28 us
  transfers between devices with their start and end apart: 3 -> 6, of which waited for: 3 -> 6; matrix products, arithmetic and copies ran while one was open for 0% -> 0% of each run, Pallas kernels for 0% -> 2%
where the time goes in v2:
time: 89.8 us; the launch traced here: 88.8 us
  Pallas kernels  25.7 us (29%)
  starting transfers between devices  22.8 us (25%)
  blocking collectives  17.7 us (20%)
  waiting for transfers between devices  14.8 us (16%)
  other arithmetic  3.39 us (4%)
  local copies, waits for them, and re-layouts  3.1 us (3%)
  between operations  1.4 us (2%)
    pallas_call x1, Pallas kernels, kernel_image(): pl.pallas_call(functools.partial(image_kernel, tile_i, tile_j), out_shape...  23.8 us
    all_to_all x1, blocking collectives, spread(): lax.all_to_all(jnp.broadcast_to(value[None], (count, *value.shape)), axes...  17.7 us
    all_to_all x1, starting transfers between devices, local(): packets = lax.all_to_all(packets, FAR + COL, 0, 0, tiled=True)  12.1 us
    all_to_all x1, starting transfers between devices, local(): partial = lax.all_to_all(partial, ('x', 'yl'), 0, 0, tiled=True)  5.89 us
    all_to_all x1, waiting for transfers between devices, local(): partial = lax.all_to_all(partial, ('x', 'yl'), 0, 0, tiled=True)  5.79 us
    ppermute x3, waiting for transfers between devices, local(): lax.ppermute(scaled, 'x', [(i, (i - step) % line) for i in range(line)])  5.08 us
    ppermute x3, starting transfers between devices, local(): lax.ppermute(scaled, 'x', [(i, (i - step) % line) for i in range(line)])  4.52 us
    all_to_all x1, waiting for transfers between devices, local(): packets = lax.all_to_all(packets, FAR + COL, 0, 0, tiled=True)  2.63 us
  transfers between devices with their start and end apart: 6, of which 6 were waited for; matrix products, arithmetic and copies ran while one was open for 0% of the time, Pallas kernels for 2%

profile of v2, /device:TPU:8, one launch (start us, length us, event | category | flops | bytes accessed | tf_op | source)
XLA Modules:
  0.0 88.8 jit_solution(15936281840297493126)
XLA Ops:
  0.6 0.0 copy-start.4
  0.6 0.7 broadcast_divide_fusion
  1.3 0.8 convert_element_type.6
  2.1 0.0 copy-done.4
  2.1 0.1 broadcast_multiply_fusion.own_ref
  2.2 0.0 copy-start.1
  2.2 0.8 broadcast_in_dim.10
  3.0 12.1 %all-to-all-start = ((bf16[64,8,384]{2,1,0:T(8,128)(2,1)}), bf16[64,8,384]{2,1,0:T(8,128)(2,1)S(1)}, u32[]{:S(2)}, u32[]{:S(2)}) async-start(bf16[64,8,384]{2,1,0:T(8,128)(2,1)} %bitcast.6), calls=%async_computation | async-start | bytes 786432 | tf_op jit(solution)/shard_map/all_to_all | solution.py:206
  15.1 2.8 %collective-permute-start = (f32[16,1024]{1,0:T(8,128)S(1)}, f32[16,1024]{1,0:T(8,128)S(1)}, u32[]{:S(2)}, u32[]{:S(2)}) collective-permute-start(f32[16,1024]{1,0:T(8,128)S(1)} %broadcast_multiply_fusion.own_ref), channel_id=1, source_target_pairs={{0,12},{4,0},{8,4},{12,8},{1,13},{5,1},{9,5},{13,9},{2,14},{6,2},{... | collective-permute-start | bytes 196616 | tf_op jit(solution)/shard_map/ppermute | solution.py:195
  17.9 0.8 collective-permute-start.1
  18.7 0.0 copy-done.1
  18.7 0.9 collective-permute-start.2
  19.6 1.5 %collective-permute-done.refs_0_ = f32[16,1024]{1,0:T(8,128)S(1)} collective-permute-done((f32[16,1024]{1,0:T(8,128)S(1)}, f32[16,1024]{1,0:T(8,128)S(1)}, u32[]{:S(2)}, u32[]{:S(2)}) %collective-permute-start) | collective-permute-done | bytes 65568 | tf_op jit(solution)/shard_map/ppermute | solution.py:195
  21.2 0.0 copy-start.5
  21.2 2.9 %collective-permute-done.1.refs_1_ = f32[16,1024]{1,0:T(8,128)S(1)} collective-permute-done((f32[16,1024]{1,0:T(8,128)S(1)}, f32[16,1024]{1,0:T(8,128)S(1)}, u32[]{:S(2)}, u32[]{:S(2)}) %collective-permute-start.1) | collective-permute-done | bytes 65568 | tf_op jit(solution)/shard_map/ppermute | solution.py:195
  24.1 0.0 copy-start.6
  24.1 0.7 collective-permute-done.2.refs_2_
  24.7 0.0 copy-start.7
  24.7 0.0 copy-done.5
  24.7 0.0 copy-done.6
  24.7 0.6 copy-done.7
  25.3 1.9 %row_features.1.rows_ref = bf16[64,4096]{1,0:T(8,128)(2,1)} custom-call(s32[1]{0:T(128)} %bitcast.2.x_ref, f32[16,1024]{1,0:T(8,128)} %copy-done.1, f32[16,1024]{1,0:T(8,128)} %copy-done.5, f32[16,1024]{1,0:T(8,128)} %copy-done.6, f32[16,1024]{1,0:T(8,128)} %copy-done.7), custom_call_target="tpu_custom_call" | custom-call | tf_op jit(solution)/shard_map/row_features/pallas_call | solution.py:57
  27.2 2.6 %all-to-all-done.packets_ref = bf16[64,8,384]{2,1,0:T(8,128)(2,1)S(1)} async-done(((bf16[64,8,384]{2,1,0:T(8,128)(2,1)}), bf16[64,8,384]{2,1,0:T(8,128)(2,1)S(1)}, u32[]{:S(2)}, u32[]{:S(2)}) %all-to-all-start) | async-done | bytes 393248 | tf_op jit(solution)/shard_map/all_to_all | solution.py:206
  29.9 0.0 copy-start
  29.9 1.0 %copy-done = bf16[64,4096]{1,0:T(8,128)(2,1)S(1)} copy-done((bf16[64,4096]{1,0:T(8,128)(2,1)S(1)}, bf16[64,4096]{1,0:T(8,128)(2,1)}, u32[]{:S(2)}) %copy-start) | copy-done | bytes 524312
  30.9 23.8 %kernel_image.1 = (f32[4,16,1024]{2,1,0:T(8,128)S(1)}, f32[4,16,1024]{2,1,0:T(8,128)S(1)}) custom-call(s32[1]{0:T(128)} %bitcast.1.core_ref, bf16[64,4096]{1,0:T(8,128)(2,1)S(1)} %copy-done, bf16[64,8,384]{2,1,0:T(8,128)(2,1)S(1)} %all-to-all-done.packets_ref), custom_call_target="tpu_custom_call" | custom-call | flops 3221225472 | bytes 4194304 | tf_op jit(solution)/shard_map/kernel_image/pallas_call | solution.py:158
  54.7 0.3 collective-permute-start.3
  55.0 1.3 %collective-permute-done.3 = f32[4,16,1024]{2,1,0:T(8,128)S(1)} collective-permute-done((f32[4,16,1024]{2,1,0:T(8,128)S(1)}, f32[4,16,1024]{2,1,0:T(8,128)S(1)}, u32[]{:S(2)}, u32[]{:S(2)}) %collective-permute-start.3) | collective-permute-done | bytes 262176 | tf_op jit(solution)/shard_map/ppermute | solution.py:209
  56.3 0.7 add.20
  57.0 0.0 copy-start.9
  57.0 5.9 %all-to-all-start.1 = ((f32[8,8,1024]{2,1,0:T(8,128)}), f32[8,8,1024]{2,1,0:T(8,128)S(1)}, u32[]{:S(2)}, u32[]{:S(2)}) async-start(f32[8,8,1024]{2,1,0:T(8,128)} %bitcast.7), calls=%async_computation.1 | async-start | bytes 524288 | tf_op jit(solution)/shard_map/all_to_all | solution.py:211
  63.6 0.0 copy-start.2
  63.6 0.0 copy-start.3
  63.6 5.8 %all-to-all-done.1 = f32[8,8,1024]{2,1,0:T(8,128)S(1)} async-done(((f32[8,8,1024]{2,1,0:T(8,128)}), f32[8,8,1024]{2,1,0:T(8,128)S(1)}, u32[]{:S(2)}, u32[]{:S(2)}) %all-to-all-start.1) | async-done | bytes 262176 | tf_op jit(solution)/shard_map/all_to_all | solution.py:211
  69.4 0.0 copy-done.9
  69.4 0.0 copy-done.2
  69.4 0.0 copy-done.3
  69.4 0.2 multiply_reduce_fusion.3
  69.6 0.1 pad_maximum_fusion
  69.7 17.7 %all_to_all.16 = f32[64,1,32]{2,1,0:T(1,128)S(1)} all-to-all(f32[64,1,32]{2,1,0:T(1,128)S(1)} %broadcast_in_dim.11), channel_id=1, replica_groups=mesh['z'=8,'yh'=2,'x'=4,'yl'=2,'core'=2] {'z','yh','x'}, dimensions={0} | all-to-all | bytes 16384 | tf_op jit(solution)/shard_map/all_to_all | solution.py:181
  87.4 0.0 copy-start.8
  87.4 0.1 reduce_sum.59
  87.4 0.1 maximum_divide_fusion
  87.5 0.6 copy-done.8
  88.1 0.7 multiply_add_fusion
  (5 shorter events, 0.1 us)
Async XLA Ops:
  0.6 1.5 %copy-start.4 = (f32[16,1024]{1,0:T(8,128)S(1)}, f32[16,1024]{1,0:T(8,128)}, u32[]{:S(2)}) copy-start(f32[16,1024]{1,0:T(8,128)} %param.7) | copy-start | bytes 196612
  2.2 16.6 %copy-start.1 = (f32[16,1024]{1,0:T(8,128)}, f32[16,1024]{1,0:T(8,128)S(1)}, u32[]{:S(2)}) copy-start(f32[16,1024]{1,0:T(8,128)S(1)} %broadcast_multiply_fusion.own_ref) | copy-start | bytes 196612
  3.0 26.9 %all-to-all-start = ((bf16[64,8,384]{2,1,0:T(8,128)(2,1)}), bf16[64,8,384]{2,1,0:T(8,128)(2,1)S(1)}, u32[]{:S(2)}, u32[]{:S(2)}) async-start(bf16[64,8,384]{2,1,0:T(8,128)(2,1)} %bitcast.6), calls=%async_computation | async-start | bytes 786432 | tf_op jit(solution)/shard_map/all_to_all | solution.py:206
  15.1 6.1 %collective-permute-start = (f32[16,1024]{1,0:T(8,128)S(1)}, f32[16,1024]{1,0:T(8,128)S(1)}, u32[]{:S(2)}, u32[]{:S(2)}) collective-permute-start(f32[16,1024]{1,0:T(8,128)S(1)} %broadcast_multiply_fusion.own_ref), channel_id=1, source_target_pairs={{0,12},{4,0},{8,4},{12,8},{1,13},{5,1},{9,5},{13,9},{2,14},{6,2},{... | collective-permute-start | bytes 196616 | tf_op jit(solution)/shard_map/ppermute | solution.py:195
  17.9 6.1 %collective-permute-start.1 = (f32[16,1024]{1,0:T(8,128)S(1)}, f32[16,1024]{1,0:T(8,128)S(1)}, u32[]{:S(2)}, u32[]{:S(2)}) collective-permute-start(f32[16,1024]{1,0:T(8,128)S(1)} %broadcast_multiply_fusion.own_ref), channel_id=1, source_target_pairs={{0,8},{4,12},{8,0},{12,4},{1,9},{5,13},{9,1},{13,5},{2,10},{6,14},... | collective-permute-start | bytes 196616 | tf_op jit(solution)/shard_map/ppermute | solution.py:195
  18.7 6.0 %collective-permute-start.2 = (f32[16,1024]{1,0:T(8,128)S(1)}, f32[16,1024]{1,0:T(8,128)S(1)}, u32[]{:S(2)}, u32[]{:S(2)}) collective-permute-start(f32[16,1024]{1,0:T(8,128)S(1)} %broadcast_multiply_fusion.own_ref), channel_id=1, source_target_pairs={{0,4},{4,8},{8,12},{12,0},{1,5},{5,9},{9,13},{13,1},{2,6},{6,10},{... | collective-permute-start | bytes 196616 | tf_op jit(solution)/shard_map/ppermute | solution.py:195
  21.2 3.6 %copy-start.5 = (f32[16,1024]{1,0:T(8,128)}, f32[16,1024]{1,0:T(8,128)S(1)}, u32[]{:S(2)}) copy-start(f32[16,1024]{1,0:T(8,128)S(1)} %collective-permute-done.refs_0_) | copy-start | bytes 196612
  24.1 0.7 copy-start.6
  24.7 0.6 copy-start.7
  29.9 1.0 %copy-start = (bf16[64,4096]{1,0:T(8,128)(2,1)S(1)}, bf16[64,4096]{1,0:T(8,128)(2,1)}, u32[]{:S(2)}) copy-start(bf16[64,4096]{1,0:T(8,128)(2,1)} %row_features.1.rows_ref) | copy-start | bytes 1572868
  54.7 1.6 %collective-permute-start.3 = (f32[4,16,1024]{2,1,0:T(8,128)S(1)}, f32[4,16,1024]{2,1,0:T(8,128)S(1)}, u32[]{:S(2)}, u32[]{:S(2)}) collective-permute-start(f32[4,16,1024]{2,1,0:T(8,128)S(1)} %get-tuple-element.6), channel_id=1, source_target_pairs={{0,1},{1,0},{2,3},{3,2},{4,5},{5,4},{6,7},{7,6},{8,9},{9,8},{10,11... | collective-permute-start | bytes 786440 | tf_op jit(solution)/shard_map/ppermute | solution.py:209
  57.0 12.4 %copy-start.9 = (f32[1024]{0:T(1024)S(1)}, f32[1024]{0:T(1024)}, u32[]{:S(2)}) copy-start(f32[1024]{0:T(1024)} %param.9) | copy-start | bytes 12292
  57.0 12.4 %all-to-all-start.1 = ((f32[8,8,1024]{2,1,0:T(8,128)}), f32[8,8,1024]{2,1,0:T(8,128)S(1)}, u32[]{:S(2)}, u32[]{:S(2)}) async-start(f32[8,8,1024]{2,1,0:T(8,128)} %bitcast.7), calls=%async_computation.1 | async-start | bytes 524288 | tf_op jit(solution)/shard_map/all_to_all | solution.py:211
  63.6 5.8 %copy-start.2 = (f32[8,1024]{1,0:T(8,128)S(1)}, f32[8,1024]{1,0:T(8,128)}, u32[]{:S(2)}) copy-start(f32[8,1024]{1,0:T(8,128)} %param.13) | copy-start | bytes 98308
  63.6 5.8 %copy-start.3 = (f32[8,1024]{1,0:T(8,128)S(1)}, f32[8,1024]{1,0:T(8,128)}, u32[]{:S(2)}) copy-start(f32[8,1024]{1,0:T(8,128)} %param.12) | copy-start | bytes 98308
  87.4 0.8 copy-start.8

commit v3 on v2

v3 whole, which is shorter than its diff:
```python
import functools
import math

import jax
import jax.numpy as jnp
from jax import lax
from jax.experimental import pallas as pl
from jax.experimental.pallas import tpu as pltpu
from jax.sharding import Mesh, PartitionSpec as P

F32 = jnp.float32
BF16 = jnp.bfloat16
KAPPA = 1.0 / math.log(2.0)
SHIFT = -1.5 * KAPPA
CONST = 0.75 * KAPPA * KAPPA
FACTOR = math.exp(1.5) / (3.0 * KAPPA * KAPPA)
TINY = 1e-30

BLK = ("z", "yh", "x")
COL = ("yl", "core")
FAR = ("z", "yh")


def split3(value):
    high = value.astype(BF16).astype(F32)
    rest = value - high
    middle = rest.astype(BF16).astype(F32)
    return high, middle, rest - middle


def stack_rows(rows, width):
    index = lax.broadcasted_iota(jnp.int32, (16, width), 0)
    total = jnp.zeros((16, width), F32)
    for place, row in enumerate(rows):
        total = jnp.where(index == place, row, total)
    return total


def row_kernel(*refs):
    count = len(refs) // 2
    for ref, out_ref in zip(refs[:count], refs[count:]):
        value = ref[...]
        norm = split3(jnp.sum(value * value, axis=0, keepdims=True))
        one = jnp.ones((1, value.shape[1]), F32)
        misc = stack_rows((*norm, one, one, one), value.shape[1])
        out_ref[...] = jnp.concatenate([*split3(value), misc], axis=0).astype(BF16)


def row_features(blocks):
    vmem = pl.BlockSpec(memory_space=pltpu.VMEM)
    return pl.pallas_call(
        row_kernel,
        out_shape=tuple(jax.ShapeDtypeStruct((64, block.shape[1]), BF16) for block in blocks),
        in_specs=[vmem] * len(blocks),
        out_specs=(vmem,) * len(blocks),
        compiler_params=pltpu.CompilerParams(vmem_limit_bytes=8 * 2**20),
        name="row_features",
    )(*blocks)


def col_kernel(place_ref, packets_ref, col_f, low):
    yl = place_ref[0]
    pieces = packets_ref.shape[0] // 2
    piece = packets_ref.shape[2] // 3

    def features(p):
        parts = [packets_ref[q * pieces + p].astype(F32) for q in range(2)]
        value = jnp.concatenate([part[:, 2 * piece :] for part in parts], axis=0)
        norm = split3(jnp.sum(value * value, axis=0, keepdims=True))
        one = jnp.ones((1, piece), F32)
        misc = stack_rows((one, one, one, *norm), piece)
        cross = -2.0 * value
        place = pl.ds(pl.multiple_of(p * piece, piece), piece)
        col_f[place, :] = jnp.concatenate([cross, cross, cross, misc], axis=0).T.astype(BF16)
        parts = [packets_ref[q * pieces + p].astype(F32) for q in (yl, 1 - yl)]
        columns = [part[:, k * piece : (k + 1) * piece] for k in range(2) for part in parts]
        low[:, place] = jnp.concatenate(columns, axis=0).astype(BF16)

    def some(index, _):
        for k in range(4):
            features(4 * index + k)
        return 0

    lax.fori_loop(0, pieces // 4, some, 0)


def col_features(place, packets):
    vmem = pl.BlockSpec(memory_space=pltpu.VMEM)
    count = packets.shape[0] * packets.shape[2] // 6
    return pl.pallas_call(
        col_kernel,
        out_shape=(jax.ShapeDtypeStruct((count, 64), BF16), jax.ShapeDtypeStruct((32, count), BF16)),
        in_specs=[pl.BlockSpec(memory_space=pltpu.SMEM), vmem],
        out_specs=(vmem, vmem),
        compiler_params=pltpu.CompilerParams(vmem_limit_bytes=8 * 2**20),
        name="col_features",
    )(place, packets)


def image_kernel(groups, tile_i, tile_j, *refs):
    rows_refs, (col_f, low), out_refs = refs[:groups], refs[groups : groups + 2], refs[groups + 2 : 2 * groups + 2]
    rows, total, dist_s, expo_s, kern_s = refs[2 * groups + 2 :]
    count_j = low.shape[1]
    width = out_refs[0].shape[1]
    count_i = groups * width
    for g in range(groups):
        rows[:, g * width : (g + 1) * width] = rows_refs[g][...]
    per = count_j // tile_j
    steps = (count_i // tile_i) * per
    per_group = width // tile_i

    def spot_i(step):
        return pl.ds(pl.multiple_of((step // per) * tile_i, tile_i), tile_i)

    def spot_j(step):
        return pl.ds(pl.multiple_of((step % per) * tile_j, tile_j), tile_j)

    def distances(step, slot):
        dist_s[slot] = jnp.dot(
            col_f[spot_j(step), :], rows[:, spot_i(step)], preferred_element_type=F32
        )

    def exponents(slot, a):
        dist = jnp.maximum(dist_s[slot, a : a + 16, :], TINY)
        expo_s[slot, a : a + 16, :] = SHIFT - dist * lax.rsqrt(dist)

    def entries(slot, a):
        t = expo_s[slot, a : a + 16, :]
        kern_s[slot, a : a + 16, :] = ((t * t + CONST) * jnp.exp2(t)).astype(BF16)

    def accumulate(step, slot):
        tile = step // per
        group = tile // per_group
        place = pl.ds(pl.multiple_of((tile % per_group) * tile_i, tile_i), tile_i)
        product = jnp.dot(low[:, spot_j(step)], kern_s[slot], preferred_element_type=F32)
        total[group, :, place] += product

    total[...] = jnp.zeros_like(total)
    kern_s[1] = jnp.zeros((tile_j, tile_i), BF16)
    distances(0, 0)
    distances(1, 1)
    for a in range(0, tile_j, 16):
        exponents(0, a)

    def one(step, slot):
        accumulate(jnp.maximum(step - 1, 0), 1 - slot)
        for a in range(0, tile_j, 16):
            entries(slot, a)
            exponents(1 - slot, a)
        distances(jnp.minimum(step + 2, steps - 1), slot)

    def four(index, _):
        for k in range(4):
            one(4 * index + k, k % 2)
        return 0

    lax.fori_loop(0, steps // 4, four, 0)
    accumulate(steps - 1, 1)
    for g in range(groups):
        out_refs[g][...] = total[g]


def kernel_image(rows, col_f, low, tile_i=256, tile_j=1024):
    groups, width, count_j = len(rows), rows[0].shape[1], low.shape[1]
    count_i = groups * width
    vmem = pl.BlockSpec(memory_space=pltpu.VMEM)
    return pl.pallas_call(
        functools.partial(image_kernel, groups, tile_i, tile_j),
        out_shape=(jax.ShapeDtypeStruct((32, width), F32),) * groups,
        in_specs=[vmem] * (groups + 2),
        out_specs=(vmem,) * groups,
        scratch_shapes=[
            pltpu.VMEM((64, count_i), BF16),
            pltpu.VMEM((groups, 32, width), F32),
            pltpu.VMEM((2, tile_j, tile_i), F32),
            pltpu.VMEM((2, tile_j, tile_i), F32),
            pltpu.VMEM((2, tile_j, tile_i), BF16),
        ],
        compiler_params=pltpu.CompilerParams(vmem_limit_bytes=24 * 2**20),
        cost_estimate=pl.CostEstimate(
            flops=2 * count_i * count_j * 96,
            bytes_accessed=4 * 1024 * 1024,
            transcendentals=2 * count_i * count_j,
        ),
        name="kernel_image",
    )(*rows, col_f, low)


def add_kernel(count, *refs):
    total = refs[0][...]
    for ref in refs[1:count]:
        total = total + ref[...]
    half = total.shape[0] // 2
    refs[count][...] = total[:half]
    refs[count + 1][...] = total[half:]


def add_parts(parts):
    vmem = pl.BlockSpec(memory_space=pltpu.VMEM)
    columns, width = parts[0].shape
    return pl.pallas_call(
        functools.partial(add_kernel, len(parts)),
        out_shape=(jax.ShapeDtypeStruct((columns // 2, width), F32),) * 2,
        in_specs=[vmem] * len(parts),
        out_specs=(vmem,) * 2,
        compiler_params=pltpu.CompilerParams(vmem_limit_bytes=8 * 2**20),
        name="add_parts",
    )(*parts)


def pack_kernel(far, place_ref, lengths_ref, points_ref, direction_ref, other_ref, scaled_ref, packets_ref):
    yl, core = place_ref[0], place_ref[1]
    dims, count = points_ref.shape
    piece = count // 4
    index = lax.broadcasted_iota(jnp.int32, (dims, 128), 0)
    lengths = jnp.ones((dims, 128), F32)
    for d in range(dims):
        lengths = jnp.where(index == d, lengths_ref[d], lengths)
    scale = ((KAPPA * math.sqrt(5.0)) / lengths)[:, :1]
    scaled_ref[...] = points_ref[...] * scale
    for q in range(2):
        here = pl.ds(pl.multiple_of((2 * q + core) * piece, piece), piece)
        half = scaled_ref[pl.ds(pl.multiple_of(yl * 8, 8), 8), here]
        packet = jnp.concatenate([direction_ref[:, here], other_ref[:, here], half], axis=1).astype(BF16)
        for n in range(far):
            packets_ref[q * far + n] = packet


def pack(far, place, lengths, points, direction, other):
    vmem = pl.BlockSpec(memory_space=pltpu.VMEM)
    smem = pl.BlockSpec(memory_space=pltpu.SMEM)
    own, count = direction.shape
    return pl.pallas_call(
        functools.partial(pack_kernel, far),
        out_shape=(
            jax.ShapeDtypeStruct(points.shape, F32),
            jax.ShapeDtypeStruct((2 * far, own, 3 * count // 4), BF16),
        ),
        in_specs=[smem, smem, vmem, vmem, vmem],
        out_specs=(vmem, vmem),
        compiler_params=pltpu.CompilerParams(vmem_limit_bytes=8 * 2**20),
        name="pack",
    )(place, lengths, points, direction, other)


def sums_kernel(scale_ref, noise_ref, direction_ref, residual_ref, solution_ref, *refs):
    parts, (image_ref, same_ref, out_ref) = refs[:-3], refs[-3:]
    direction, residual = direction_ref[...], residual_ref[...]
    total = parts[0][...]
    for part in parts[1:]:
        total = total + part[...]
    image = (FACTOR * scale_ref[0]) * total + noise_ref[...] * direction
    image_ref[...] = image
    same_ref[...] = solution_ref[...]
    own = direction.shape[0]
    lane = lax.broadcasted_iota(jnp.int32, (own, 128), 1)
    row = lax.broadcasted_iota(jnp.int32, (own, 128), 0)
    sums = jnp.zeros((own, 128), F32)
    for k, term in enumerate((residual * residual, direction * image, residual * image, image * image)):
        sums = jnp.where(lane == k * own + row, jnp.sum(term, axis=1, keepdims=True), sums)
    out_ref[...] = jnp.broadcast_to(jnp.sum(sums, axis=0, keepdims=True), out_ref.shape)


def column_sums(scale, parts, noise, direction, residual, solution, copies):
    vmem = pl.BlockSpec(memory_space=pltpu.VMEM)
    block = jax.ShapeDtypeStruct(direction.shape, F32)
    return pl.pallas_call(
        sums_kernel,
        out_shape=(block, block, jax.ShapeDtypeStruct((copies, 128), F32)),
        in_specs=[pl.BlockSpec(memory_space=pltpu.SMEM)] + [vmem] * (4 + len(parts)),
        out_specs=(vmem,) * 3,
        compiler_params=pltpu.CompilerParams(vmem_limit_bytes=8 * 2**20),
        name="column_sums",
    )(scale, noise, direction, residual, solution, *parts)


def local(points, lengths, noise, outscale, solution, residual, direction):
    far, line = lax.axis_size(FAR), lax.axis_size("x")
    own, count = direction.shape
    swap = [(0, 1), (1, 0)]

    place = jnp.stack([lax.axis_index("yl"), lax.axis_index("core")])
    other = lax.ppermute(direction, "core", swap)
    scaled, packets = pack(far, place, lengths, points, direction, other)
    packets = lax.all_to_all(packets, ("yl", *FAR), 0, 0, tiled=True)
    blocks = [scaled] + [
        lax.ppermute(scaled, "x", [(i, (i - step) % line) for i in range(line)])
        for step in range(1, line)
    ]
    rows = row_features(blocks)

    def send(value, step):
        return lax.ppermute(value, "x", [(i, (i + step) % line) for i in range(line)])

    columns = col_features(place, packets)
    image3, image2, image1 = kernel_image((rows[3], rows[2], rows[1]), *columns)
    image3, image2, image1 = send(image3, 3), send(image2, 2), send(image1, 1)
    (image0,) = kernel_image((rows[0],), *columns)
    keep, rest = add_parts((image0, image1, image2, image3))
    keep, rest = add_parts((keep, lax.ppermute(rest, "core", swap)))
    parts = [keep, lax.ppermute(rest, "yl", swap)]
    image, solution, sums = column_sums(
        outscale, parts, noise[None, :], direction, residual, solution, lax.axis_size(BLK)
    )
    sums = lax.all_to_all(sums, BLK, 0, 0, tiled=True)
    sums = jnp.sum(sums, axis=0)[: 4 * own].reshape(4, own)
    norm_now, curve, mixed, square = sums[0], sums[1], sums[2], sums[3]
    alpha = norm_now / curve
    norm_next = jnp.maximum(norm_now - alpha * (2.0 * mixed - alpha * square), 0.0)
    solution_next = solution + alpha[:, None] * direction
    residual_next = residual - alpha[:, None] * image
    direction_next = residual_next + (norm_next / norm_now)[:, None] * direction
    return (solution_next, residual_next, direction_next)


def solution(mesh):
    fine = Mesh(mesh.devices.reshape(8, 2, 4, 2, 2), (*BLK, *COL))
    in_specs = (
        P(None, BLK),
        P(),
        P(BLK),
        P(),
        P(COL, BLK),
        P(COL, BLK),
        P(COL, BLK),
    )
    out_specs = (P(COL, BLK), P(COL, BLK), P(COL, BLK))
    return jax.shard_map(local, mesh=fine, in_specs=in_specs, out_specs=out_specs, check_vma=False)
```

time: 89.8 us -> 84.6 us (0.942)
  other arithmetic: 3.39 us -> 0.96 us
  local copies, waits for them, and re-layouts: 3.1 us -> 1.62 us
    ppermute x1 -> x6, starting transfers between devices: 0.29 us -> 7.32 us  [the longest x3 5.73 us: send(): lax.ppermute(value, 'x', [(i, (i + step) % line) for i in range(line)])]
    all_to_all x2 -> x1, starting transfers between devices: 18 us -> 11.7 us  [local(): packets = lax.all_to_all(packets, ('yl', *FAR), 0, 0, tiled=True)]
    all_to_all x2 -> x1, waiting for transfers between devices: 8.42 us -> 4.85 us  [local(): packets = lax.all_to_all(packets, ('yl', *FAR), 0, 0, tiled=True)]
    ppermute x1 -> x6, waiting for transfers between devices: 1.34 us -> 4.51 us  [the longest x1 1.95 us: local(): parts = [keep, lax.ppermute(rest, 'yl', swap)]]
    unnamed x20 -> x14, local copies, waits for them, and re-layouts: 2.28 us -> 1.62 us
    pallas_call x2 -> x8, Pallas kernels: 25.7 us -> 25.4 us  [the longest x2 22.7 us: kernel_image(): pl.pallas_call(functools.partial(image_kernel, groups, tile_i, tile_j), o...]
  transfers between devices with their start and end apart: 6 -> 10, of which waited for: 6 -> 7; matrix products, arithmetic and copies ran while one was open for 0% -> 0% of each run, Pallas kernels for 2% -> 7%
where the time goes in v3:
time: 84.6 us; the launch traced here: 84.2 us
  Pallas kernels  25.4 us (30%)
  starting transfers between devices  23.5 us (28%)
  blocking collectives  17.1 us (20%)
  waiting for transfers between devices  14.1 us (17%)
  local copies, waits for them, and re-layouts  1.62 us (2%)
  between operations  1.41 us (2%)
  other arithmetic  0.96 us (1%)
    pallas_call x2, Pallas kernels, kernel_image(): pl.pallas_call(functools.partial(image_kernel, groups, tile_i, tile_j), o...  22.7 us
    all_to_all x1, blocking collectives, local(): sums = lax.all_to_all(sums, BLK, 0, 0, tiled=True)  17.1 us
    all_to_all x1, starting transfers between devices, local(): packets = lax.all_to_all(packets, ('yl', *FAR), 0, 0, tiled=True)  11.7 us
    ppermute x3, starting transfers between devices, send(): lax.ppermute(value, 'x', [(i, (i + step) % line) for i in range(line)])  5.73 us
    all_to_all x1, waiting for transfers between devices, local(): packets = lax.all_to_all(packets, ('yl', *FAR), 0, 0, tiled=True)  4.85 us
    ppermute x3, waiting for transfers between devices, local(): lax.ppermute(scaled, 'x', [(i, (i - step) % line) for i in range(line)])  4.78 us
    ppermute x3, starting transfers between devices, local(): lax.ppermute(scaled, 'x', [(i, (i - step) % line) for i in range(line)])  4.52 us
    ppermute x1, waiting for transfers between devices, local(): parts = [keep, lax.ppermute(rest, 'yl', swap)]  1.95 us
  transfers between devices with their start and end apart: 10, of which 7 were waited for; matrix products, arithmetic and copies ran while one was open for 0% of the time, Pallas kernels for 7%

profile of v3, /device:TPU:8, one launch (start us, length us, event | category | flops | bytes accessed | tf_op | source)
XLA Modules:
  0.0 84.2 jit_solution(387834415224002884)
XLA Ops:
  0.6 0.1 collective-permute-start
  0.7 0.0 copy-start.6
  0.7 0.1 pad_add_fusion.place_ref
  0.8 1.3 %collective-permute-done.other_ref = f32[8,1024]{1,0:T(8,128)S(1)} collective-permute-done((f32[8,1024]{1,0:T(8,128)}, f32[8,1024]{1,0:T(8,128)S(1)}, u32[]{:S(2)}, u32[]{:S(2)}) %collective-permute-start) | collective-permute-done | bytes 32800 | tf_op jit(solution)/shard_map/ppermute | solution.py:283
  2.1 0.0 copy-done.6
  2.1 0.0 copy-start
  2.1 0.8 copy-done
  2.9 0.0 copy-start.3
  2.9 0.8 copy-done.3
  3.7 1.3 %pack.1 = (f32[16,1024]{1,0:T(8,128)S(1)}, bf16[32,8,768]{2,1,0:T(8,128)(2,1)}) custom-call(s32[2]{0:T(128)S(1)} %pad_add_fusion.place_ref, f32[16]{0:T(128)S(1)} %copy-done.6, f32[16,1024]{1,0:T(8,128)S(1)} %copy-done.3, f32[8,1024]{1,0:T(8,128)S(1)} %copy-done, f32[8,1024]{1,0:T(8,128)S(1)} %collective-permute-done.other_ref), custom_call_target="tpu_custom_call" | custom-call | tf_op jit(solution)/shard_map/pack/pallas_call | solution.py:233
  5.1 11.7 %all-to-all-start = ((bf16[32,8,768]{2,1,0:T(8,128)(2,1)}), bf16[32,8,768]{2,1,0:T(8,128)(2,1)S(1)}, u32[]{:S(2)}, u32[]{:S(2)}) async-start(bf16[32,8,768]{2,1,0:T(8,128)(2,1)} %get-tuple-element.23), calls=%async_computation | async-start | bytes 786432 | tf_op jit(solution)/shard_map/all_to_all | solution.py:285
  16.8 2.8 %collective-permute-start.1 = (f32[16,1024]{1,0:T(8,128)S(1)}, f32[16,1024]{1,0:T(8,128)S(1)}, u32[]{:S(2)}, u32[]{:S(2)}) collective-permute-start(f32[16,1024]{1,0:T(8,128)S(1)} %get-tuple-element.21.refs_0_), channel_id=1, source_target_pairs={{0,12},{4,0},{8,4},{12,8},{1,13},{5,1},{9,5},{13,9},{2,14},{6,2},{... | collective-permute-start | bytes 196616 | tf_op jit(solution)/shard_map/ppermute | solution.py:287
  19.6 0.8 collective-permute-start.2
  20.4 0.9 %collective-permute-start.3 = (f32[16,1024]{1,0:T(8,128)S(1)}, f32[16,1024]{1,0:T(8,128)S(1)}, u32[]{:S(2)}, u32[]{:S(2)}) collective-permute-start(f32[16,1024]{1,0:T(8,128)S(1)} %get-tuple-element.21.refs_0_), channel_id=1, source_target_pairs={{0,4},{4,8},{8,12},{12,0},{1,5},{5,9},{9,13},{13,1},{2,6},{6,10},{... | collective-permute-start | bytes 196616 | tf_op jit(solution)/shard_map/ppermute | solution.py:287
  21.3 0.3 collective-permute-done.1.refs_1_
  21.6 3.8 %collective-permute-done.2.refs_2_ = f32[16,1024]{1,0:T(8,128)S(1)} collective-permute-done((f32[16,1024]{1,0:T(8,128)S(1)}, f32[16,1024]{1,0:T(8,128)S(1)}, u32[]{:S(2)}, u32[]{:S(2)}) %collective-permute-start.2) | collective-permute-done | bytes 65568 | tf_op jit(solution)/shard_map/ppermute | solution.py:287
  25.4 0.7 collective-permute-done.3.refs_3_
  26.1 0.2 row_features.1
  26.3 4.8 %all-to-all-done.packets_ref = bf16[32,8,768]{2,1,0:T(8,128)(2,1)S(1)} async-done(((bf16[32,8,768]{2,1,0:T(8,128)(2,1)}), bf16[32,8,768]{2,1,0:T(8,128)(2,1)S(1)}, u32[]{:S(2)}, u32[]{:S(2)}) %all-to-all-start) | async-done | bytes 393248 | tf_op jit(solution)/shard_map/all_to_all | solution.py:285
  31.1 1.2 %col_features.1 = (bf16[4096,64]{1,0:T(8,128)(2,1)S(1)}, bf16[32,4096]{1,0:T(8,128)(2,1)S(1)}) custom-call(s32[2]{0:T(128)S(1)} %pad_add_fusion.place_ref, bf16[32,8,768]{2,1,0:T(8,128)(2,1)S(1)} %all-to-all-done.packets_ref), custom_call_target="tpu_custom_call" | custom-call | tf_op jit(solution)/shard_map/col_features/pallas_call | solution.py:90
  32.3 16.7 %kernel_image.3 = (f32[32,1024]{1,0:T(8,128)S(1)}, f32[32,1024]{1,0:T(8,128)S(1)}, f32[32,1024]{1,0:T(8,128)S(1)}) custom-call(bf16[64,1024]{1,0:T(8,128)(2,1)S(1)} %get-tuple-element.26.refs_0_, bf16[64,1024]{1,0:T(8,128)(2,1)S(1)} %get-tuple-element.27.refs_1_, bf16[64,1024]{1,0:T(8,128)(2,1)S(1)} %get-tuple-element.28.refs_2_, ...), custom_call_target="tpu_custom_call" | custom-call | flops 2415919104 | bytes 4194304 | tf_op jit(solution)/shard_map/kernel_image/pallas_call | solution.py:167
  49.0 1.6 %collective-permute-start.4 = (f32[32,1024]{1,0:T(8,128)S(1)}, f32[32,1024]{1,0:T(8,128)S(1)}, u32[]{:S(2)}, u32[]{:S(2)}) collective-permute-start(f32[32,1024]{1,0:T(8,128)S(1)} %get-tuple-element.29), channel_id=1, source_target_pairs={{0,4},{4,8},{8,12},{12,0},{1,5},{5,9},{9,13},{13,1},{2,6},{6,10},{... | collective-permute-start | bytes 393224 | tf_op jit(solution)/shard_map/ppermute | solution.py:293
  50.5 2.7 %collective-permute-start.5 = (f32[32,1024]{1,0:T(8,128)S(1)}, f32[32,1024]{1,0:T(8,128)S(1)}, u32[]{:S(2)}, u32[]{:S(2)}) collective-permute-start(f32[32,1024]{1,0:T(8,128)S(1)} %get-tuple-element.30), channel_id=1, source_target_pairs={{0,8},{4,12},{8,0},{12,4},{1,9},{5,13},{9,1},{13,5},{2,10},{6,14},... | collective-permute-start | bytes 393224 | tf_op jit(solution)/shard_map/ppermute | solution.py:293
  53.3 1.4 %collective-permute-start.6 = (f32[32,1024]{1,0:T(8,128)S(1)}, f32[32,1024]{1,0:T(8,128)S(1)}, u32[]{:S(2)}, u32[]{:S(2)}) collective-permute-start(f32[32,1024]{1,0:T(8,128)S(1)} %get-tuple-element.31), channel_id=1, source_target_pairs={{0,12},{4,0},{8,4},{12,8},{1,13},{5,1},{9,5},{13,9},{2,14},{6,2},{... | collective-permute-start | bytes 393224 | tf_op jit(solution)/shard_map/ppermute | solution.py:293
  54.7 6.0 %kernel_image.2.refs_0_ = f32[32,1024]{1,0:T(8,128)S(1)} custom-call(bf16[64,1024]{1,0:T(8,128)(2,1)S(1)} %get-tuple-element.22.refs_0_, bf16[4096,64]{1,0:T(8,128)(2,1)S(1)} %get-tuple-element.24.refs_1_.refs_3_, bf16[32,4096]{1,0:T(8,128)(2,1)S(1)} %get-tuple-element.25.refs_2_.refs_4_), custom_call_target="tpu_custom_call" | custom-call | flops 805306368 | bytes 4194304 | tf_op jit(solution)/shard_map/kernel_image/pallas_call | solution.py:167
  60.7 0.0 collective-permute-done.4.refs_1_
  60.7 0.0 collective-permute-done.5.refs_2_
  60.7 0.0 collective-permute-done.6.refs_3_
  60.7 0.1 collective-permute-start.7
  60.8 1.2 %collective-permute-done.7.refs_1_ = f32[16,1024]{1,0:T(8,128)S(1)} collective-permute-done((f32[16,1024]{1,0:T(8,128)S(1)}, f32[16,1024]{1,0:T(8,128)S(1)}, u32[]{:S(2)}, u32[]{:S(2)}) %collective-permute-start.7) | collective-permute-done | bytes 65568 | tf_op jit(solution)/shard_map/ppermute | solution.py:300
  62.1 0.0 copy-start.1
  62.1 0.0 copy-start.2
  62.1 0.0 copy-start.4
  62.1 0.0 copy-start.5
  62.1 1.4 %collective-permute-start.8 = (f32[8,1024]{1,0:T(8,128)S(1)}, f32[8,1024]{1,0:T(8,128)S(1)}, u32[]{:S(2)}, u32[]{:S(2)}) collective-permute-start(f32[8,1024]{1,0:T(8,128)S(1)} %get-tuple-element.35), channel_id=1, source_target_pairs={{0,2},{2,0},{1,3},{3,1},{4,6},{6,4},{5,7},{7,5},{8,10},{10,8},{9,1... | collective-permute-start | bytes 98312 | tf_op jit(solution)/shard_map/ppermute | solution.py:301
  64.2 1.9 %collective-permute-done.8.refs_1_ = f32[8,1024]{1,0:T(8,128)S(1)} collective-permute-done((f32[8,1024]{1,0:T(8,128)S(1)}, f32[8,1024]{1,0:T(8,128)S(1)}, u32[]{:S(2)}, u32[]{:S(2)}) %collective-permute-start.8) | collective-permute-done | bytes 32800 | tf_op jit(solution)/shard_map/ppermute | solution.py:301
  66.1 0.0 copy-done.1
  66.1 0.0 copy-done.2
  66.1 0.0 copy-done.4
  66.1 0.0 copy-done.5
  66.1 0.1 column_sums.1
  66.2 17.1 %all_to_all.14 = f32[64,1,128]{2,1,0:T(1,128)S(1)} all-to-all(f32[64,1,128]{2,1,0:T(1,128)S(1)} %bitcast.6), channel_id=1, replica_groups=mesh['z'=8,'yh'=2,'x'=4,'yl'=2,'core'=2] {'z','yh','x'}, dimensions={0} | all-to-all | bytes 65536 | tf_op jit(solution)/shard_map/all_to_all | solution.py:305
  83.3 0.1 reduce_sum.9
  83.4 0.1 maximum_divide_fusion
  83.5 0.7 multiply_add_fusion
  (2 shorter events, 0.0 us)
Async XLA Ops:
  0.6 1.5 %collective-permute-start = (f32[8,1024]{1,0:T(8,128)}, f32[8,1024]{1,0:T(8,128)S(1)}, u32[]{:S(2)}, u32[]{:S(2)}) collective-permute-start(f32[8,1024]{1,0:T(8,128)} %direction_ref.3), channel_id=1, source_target_pairs={{0,1},{1,0},{2,3},{3,2},{4,5},{5,4},{6,7},{7,6},{8,9},{9,8},{10,11... | collective-permute-start | bytes 98312 | tf_op jit(solution)/shard_map/ppermute | solution.py:283
  0.7 1.4 %copy-start.6 = (f32[16]{0:T(128)S(1)}, f32[16]{0:T(128)}, u32[]{:S(2)}) copy-start(f32[16]{0:T(128)} %lengths_ref.1) | copy-start | bytes 196
  2.1 0.8 copy-start
  2.9 0.8 copy-start.3
  5.1 26.0 %all-to-all-start = ((bf16[32,8,768]{2,1,0:T(8,128)(2,1)}), bf16[32,8,768]{2,1,0:T(8,128)(2,1)S(1)}, u32[]{:S(2)}, u32[]{:S(2)}) async-start(bf16[32,8,768]{2,1,0:T(8,128)(2,1)} %get-tuple-element.23), calls=%async_computation | async-start | bytes 786432 | tf_op jit(solution)/shard_map/all_to_all | solution.py:285
  16.8 4.8 %collective-permute-start.1 = (f32[16,1024]{1,0:T(8,128)S(1)}, f32[16,1024]{1,0:T(8,128)S(1)}, u32[]{:S(2)}, u32[]{:S(2)}) collective-permute-start(f32[16,1024]{1,0:T(8,128)S(1)} %get-tuple-element.21.refs_0_), channel_id=1, source_target_pairs={{0,12},{4,0},{8,4},{12,8},{1,13},{5,1},{9,5},{13,9},{2,14},{6,2},{... | collective-permute-start | bytes 196616 | tf_op jit(solution)/shard_map/ppermute | solution.py:287
  19.6 5.8 %collective-permute-start.2 = (f32[16,1024]{1,0:T(8,128)S(1)}, f32[16,1024]{1,0:T(8,128)S(1)}, u32[]{:S(2)}, u32[]{:S(2)}) collective-permute-start(f32[16,1024]{1,0:T(8,128)S(1)} %get-tuple-element.21.refs_0_), channel_id=1, source_target_pairs={{0,8},{4,12},{8,0},{12,4},{1,9},{5,13},{9,1},{13,5},{2,10},{6,14},... | collective-permute-start | bytes 196616 | tf_op jit(solution)/shard_map/ppermute | solution.py:287
  20.4 5.7 %collective-permute-start.3 = (f32[16,1024]{1,0:T(8,128)S(1)}, f32[16,1024]{1,0:T(8,128)S(1)}, u32[]{:S(2)}, u32[]{:S(2)}) collective-permute-start(f32[16,1024]{1,0:T(8,128)S(1)} %get-tuple-element.21.refs_0_), channel_id=1, source_target_pairs={{0,4},{4,8},{8,12},{12,0},{1,5},{5,9},{9,13},{13,1},{2,6},{6,10},{... | collective-permute-start | bytes 196616 | tf_op jit(solution)/shard_map/ppermute | solution.py:287
  49.0 11.7 %collective-permute-start.4 = (f32[32,1024]{1,0:T(8,128)S(1)}, f32[32,1024]{1,0:T(8,128)S(1)}, u32[]{:S(2)}, u32[]{:S(2)}) collective-permute-start(f32[32,1024]{1,0:T(8,128)S(1)} %get-tuple-element.29), channel_id=1, source_target_pairs={{0,4},{4,8},{8,12},{12,0},{1,5},{5,9},{9,13},{13,1},{2,6},{6,10},{... | collective-permute-start | bytes 393224 | tf_op jit(solution)/shard_map/ppermute | solution.py:293
  50.5 10.1 %collective-permute-start.5 = (f32[32,1024]{1,0:T(8,128)S(1)}, f32[32,1024]{1,0:T(8,128)S(1)}, u32[]{:S(2)}, u32[]{:S(2)}) collective-permute-start(f32[32,1024]{1,0:T(8,128)S(1)} %get-tuple-element.30), channel_id=1, source_target_pairs={{0,8},{4,12},{8,0},{12,4},{1,9},{5,13},{9,1},{13,5},{2,10},{6,14},... | collective-permute-start | bytes 393224 | tf_op jit(solution)/shard_map/ppermute | solution.py:293
  53.3 7.4 %collective-permute-start.6 = (f32[32,1024]{1,0:T(8,128)S(1)}, f32[32,1024]{1,0:T(8,128)S(1)}, u32[]{:S(2)}, u32[]{:S(2)}) collective-permute-start(f32[32,1024]{1,0:T(8,128)S(1)} %get-tuple-element.31), channel_id=1, source_target_pairs={{0,12},{4,0},{8,4},{12,8},{1,13},{5,1},{9,5},{13,9},{2,14},{6,2},{... | collective-permute-start | bytes 393224 | tf_op jit(solution)/shard_map/ppermute | solution.py:293
  60.7 1.3 %collective-permute-start.7 = (f32[16,1024]{1,0:T(8,128)S(1)}, f32[16,1024]{1,0:T(8,128)S(1)}, u32[]{:S(2)}, u32[]{:S(2)}) collective-permute-start(f32[16,1024]{1,0:T(8,128)S(1)} %get-tuple-element.33), channel_id=1, source_target_pairs={{0,1},{1,0},{2,3},{3,2},{4,5},{5,4},{6,7},{7,6},{8,9},{9,8},{10,11... | collective-permute-start | bytes 196616 | tf_op jit(solution)/shard_map/ppermute | solution.py:300
  62.1 4.0 %copy-start.1 = (f32[8,1024]{1,0:T(8,128)S(1)}, f32[8,1024]{1,0:T(8,128)}, u32[]{:S(2)}) copy-start(f32[8,1024]{1,0:T(8,128)} %direction_ref.3) | copy-start | bytes 98308
  62.1 4.0 %copy-start.2 = (f32[8,1024]{1,0:T(8,128)S(1)}, f32[8,1024]{1,0:T(8,128)}, u32[]{:S(2)}) copy-start(f32[8,1024]{1,0:T(8,128)} %residual_ref.1) | copy-start | bytes 98308
  62.1 4.0 %copy-start.4 = (f32[8,1024]{1,0:T(8,128)S(1)}, f32[8,1024]{1,0:T(8,128)}, u32[]{:S(2)}) copy-start(f32[8,1024]{1,0:T(8,128)} %solution_ref.1) | copy-start | bytes 98308
  62.1 4.0 %copy-start.5 = (f32[1024]{0:T(1024)S(1)}, f32[1024]{0:T(1024)}, u32[]{:S(2)}) copy-start(f32[1024]{0:T(1024)} %param.9) | copy-start | bytes 12292
  62.1 4.0 %collective-permute-start.8 = (f32[8,1024]{1,0:T(8,128)S(1)}, f32[8,1024]{1,0:T(8,128)S(1)}, u32[]{:S(2)}, u32[]{:S(2)}) collective-permute-start(f32[8,1024]{1,0:T(8,128)S(1)} %get-tuple-element.35), channel_id=1, source_target_pairs={{0,2},{2,0},{1,3},{3,1},{4,6},{6,4},{5,7},{7,5},{8,10},{10,8},{9,1... | collective-permute-start | bytes 98312 | tf_op jit(solution)/shard_map/ppermute | solution.py:301

commit v4 on v3

--- a/solution.py
+++ b/solution.py
@@ -18,7 +18,7 @@
 
 BLK = ("z", "yh", "x")
 COL = ("yl", "core")
-FAR = ("z", "yh")
+FAR = ("z",)
 
 
 def split3(value):
@@ -97,14 +97,19 @@
     )(place, packets)
 
 
-def image_kernel(groups, tile_i, tile_j, *refs):
-    rows_refs, (col_f, low), out_refs = refs[:groups], refs[groups : groups + 2], refs[groups + 2 : 2 * groups + 2]
-    rows, total, dist_s, expo_s, kern_s = refs[2 * groups + 2 :]
-    count_j = low.shape[1]
+def image_kernel(groups, sets, tile_i, tile_j, more, *refs):
+    rows_refs, refs = refs[:groups], refs[groups:]
+    col_refs, low_refs, refs = refs[:sets], refs[sets : 2 * sets], refs[2 * sets :]
+    start_refs, refs = refs[: groups * more], refs[groups * more :]
+    out_refs, (rows, col_f, low, total, dist_s, expo_s, kern_s) = refs[:groups], refs[groups:]
+    part_j, count_j = low_refs[0].shape[1], low.shape[1]
     width = out_refs[0].shape[1]
     count_i = groups * width
     for g in range(groups):
         rows[:, g * width : (g + 1) * width] = rows_refs[g][...]
+    for k in range(sets):
+        col_f[k * part_j : (k + 1) * part_j, :] = col_refs[k][...]
+        low[:, k * part_j : (k + 1) * part_j] = low_refs[k][...]
     per = count_j // tile_j
     steps = (count_i // tile_i) * per
     per_group = width // tile_i
@@ -135,7 +140,8 @@
         product = jnp.dot(low[:, spot_j(step)], kern_s[slot], preferred_element_type=F32)
         total[group, :, place] += product
 
-    total[...] = jnp.zeros_like(total)
+    for g in range(groups):
+        total[g] = start_refs[g][...] if more else jnp.zeros_like(total[g])
     kern_s[1] = jnp.zeros((tile_j, tile_i), BF16)
     distances(0, 0)
     distances(1, 1)
@@ -160,17 +166,20 @@
         out_refs[g][...] = total[g]
 
 
-def kernel_image(rows, col_f, low, tile_i=256, tile_j=1024):
-    groups, width, count_j = len(rows), rows[0].shape[1], low.shape[1]
-    count_i = groups * width
-    vmem = pl.BlockSpec(memory_space=pltpu.VMEM)
-    return pl.pallas_call(
-        functools.partial(image_kernel, groups, tile_i, tile_j),
+def kernel_image(rows, columns, start=(), tile_i=256, tile_j=1024):
+    cols, lows = zip(*columns)
+    groups, sets, width = len(rows), len(cols), rows[0].shape[1]
+    count_i, count_j = groups * width, sets * lows[0].shape[1]
+    vmem = pl.BlockSpec(memory_space=pltpu.VMEM)
+    return pl.pallas_call(
+        functools.partial(image_kernel, groups, sets, tile_i, tile_j, len(start) > 0),
         out_shape=(jax.ShapeDtypeStruct((32, width), F32),) * groups,
-        in_specs=[vmem] * (groups + 2),
+        in_specs=[vmem] * (groups + 2 * sets + len(start)),
         out_specs=(vmem,) * groups,
         scratch_shapes=[
             pltpu.VMEM((64, count_i), BF16),
+            pltpu.VMEM((count_j, 64), BF16),
+            pltpu.VMEM((32, count_j), BF16),
             pltpu.VMEM((groups, 32, width), F32),
             pltpu.VMEM((2, tile_j, tile_i), F32),
             pltpu.VMEM((2, tile_j, tile_i), F32),
@@ -183,7 +192,7 @@
             transcendentals=2 * count_i * count_j,
         ),
         name="kernel_image",
-    )(*rows, col_f, low)
+    )(*rows, *cols, *lows, *start)
 
 
 def add_kernel(count, *refs):
@@ -208,39 +217,55 @@
     )(*parts)
 
 
-def pack_kernel(far, place_ref, lengths_ref, points_ref, direction_ref, other_ref, scaled_ref, packets_ref):
-    yl, core = place_ref[0], place_ref[1]
-    dims, count = points_ref.shape
-    piece = count // 4
+def prepare_kernel(lengths_ref, points_ref, direction_ref, scaled_ref, low_ref):
+    dims = points_ref.shape[0]
     index = lax.broadcasted_iota(jnp.int32, (dims, 128), 0)
     lengths = jnp.ones((dims, 128), F32)
     for d in range(dims):
         lengths = jnp.where(index == d, lengths_ref[d], lengths)
     scale = ((KAPPA * math.sqrt(5.0)) / lengths)[:, :1]
     scaled_ref[...] = points_ref[...] * scale
+    low_ref[...] = direction_ref[...].astype(BF16)
+
+
+def prepare(lengths, points, direction):
+    vmem = pl.BlockSpec(memory_space=pltpu.VMEM)
+    return pl.pallas_call(
+        prepare_kernel,
+        out_shape=(
+            jax.ShapeDtypeStruct(points.shape, F32),
+            jax.ShapeDtypeStruct(direction.shape, BF16),
+        ),
+        in_specs=[pl.BlockSpec(memory_space=pltpu.SMEM), vmem, vmem],
+        out_specs=(vmem, vmem),
+        compiler_params=pltpu.CompilerParams(vmem_limit_bytes=8 * 2**20),
+        name="prepare",
+    )(lengths, points, direction)
+
+
+def pack_kernel(far, place_ref, scaled_ref, low_ref, other_ref, packets_ref):
+    yl, core = place_ref[0], place_ref[1]
+    piece = low_ref.shape[1] // 4
     for q in range(2):
         here = pl.ds(pl.multiple_of((2 * q + core) * piece, piece), piece)
         half = scaled_ref[pl.ds(pl.multiple_of(yl * 8, 8), 8), here]
-        packet = jnp.concatenate([direction_ref[:, here], other_ref[:, here], half], axis=1).astype(BF16)
+        parts = [low_ref[:, here], other_ref[:, here].astype(BF16), half.astype(BF16)]
+        packet = jnp.concatenate(parts, axis=1)
         for n in range(far):
             packets_ref[q * far + n] = packet
 
 
-def pack(far, place, lengths, points, direction, other):
-    vmem = pl.BlockSpec(memory_space=pltpu.VMEM)
-    smem = pl.BlockSpec(memory_space=pltpu.SMEM)
-    own, count = direction.shape
+def pack(far, place, scaled, low, other):
+    vmem = pl.BlockSpec(memory_space=pltpu.VMEM)
+    own, count = low.shape
     return pl.pallas_call(
         functools.partial(pack_kernel, far),
-        out_shape=(
-            jax.ShapeDtypeStruct(points.shape, F32),
-            jax.ShapeDtypeStruct((2 * far, own, 3 * count // 4), BF16),
-        ),
-        in_specs=[smem, smem, vmem, vmem, vmem],
-        out_specs=(vmem, vmem),
+        out_shape=jax.ShapeDtypeStruct((2 * far, own, 3 * count // 4), BF16),
+        in_specs=[pl.BlockSpec(memory_space=pltpu.SMEM), vmem, vmem, vmem],
+        out_specs=vmem,
         compiler_params=pltpu.CompilerParams(vmem_limit_bytes=8 * 2**20),
         name="pack",
-    )(place, lengths, points, direction, other)
+    )(place, scaled, low, other)
 
 
 def sums_kernel(scale_ref, noise_ref, direction_ref, residual_ref, solution_ref, *refs):
@@ -281,7 +306,8 @@
 
     place = jnp.stack([lax.axis_index("yl"), lax.axis_index("core")])
     other = lax.ppermute(direction, "core", swap)
-    scaled, packets = pack(far, place, lengths, points, direction, other)
+    scaled, low = prepare(lengths, points, direction)
+    packets = pack(far, place, scaled, low, other)
     packets = lax.all_to_all(packets, ("yl", *FAR), 0, 0, tiled=True)
     blocks = [scaled] + [
         lax.ppermute(scaled, "x", [(i, (i - step) % line) for i in range(line)])
@@ -292,10 +318,13 @@
     def send(value, step):
         return lax.ppermute(value, "x", [(i, (i + step) % line) for i in range(line)])
 
-    columns = col_features(place, packets)
-    image3, image2, image1 = kernel_image((rows[3], rows[2], rows[1]), *columns)
+    packets, *rows = lax.optimization_barrier((packets, *rows))
+    near = col_features(place, packets)
+    others = kernel_image((rows[3], rows[2], rows[1]), (near,))
+    distant = col_features(place, lax.ppermute(packets, "yh", swap))
+    image3, image2, image1 = kernel_image((rows[3], rows[2], rows[1]), (distant,), others)
     image3, image2, image1 = send(image3, 3), send(image2, 2), send(image1, 1)
-    (image0,) = kernel_image((rows[0],), *columns)
+    (image0,) = kernel_image((rows[0],), (near, distant))
     keep, rest = add_parts((image0, image1, image2, image3))
     keep, rest = add_parts((keep, lax.ppermute(rest, "core", swap)))
     parts = [keep, lax.ppermute(rest, "yl", swap)]

time: 84.6 us -> 83.6 us (0.988)
  waiting for transfers between devices: 14.1 us -> 5.82 us
  blocking collectives: 17.1 us -> 20.2 us
  Pallas kernels: 25.4 us -> 27.3 us
  starting transfers between devices: 23.5 us -> 25.3 us
    all_to_all x1, waiting for transfers between devices: 4.85 us -> 0.01 us  [local(): packets = lax.all_to_all(packets, ('yl', *FAR), 0, 0, tiled=True)]
    all_to_all x1, blocking collectives: 17.1 us -> 20.2 us  [local(): sums = lax.all_to_all(sums, BLK, 0, 0, tiled=True)]
    ppermute x0 -> x1, starting transfers between devices: none -> 2.38 us  [local(): distant = col_features(place, lax.ppermute(packets, 'yh', swap))]
    ppermute x3, waiting for transfers between devices: 4.78 us -> 2.83 us  [local(): lax.ppermute(scaled, 'x', [(i, (i - step) % line) for i in range(line)])]
    all_to_all x1, starting transfers between devices: 11.7 us -> 9.94 us  [local(): packets = lax.all_to_all(packets, ('yl', *FAR), 0, 0, tiled=True)]
    ppermute x1, waiting for transfers between devices: 1.31 us -> 0.01 us  [local(): other = lax.ppermute(direction, 'core', swap)]
    pallas_call x3 -> x5, Pallas kernels: 24 us -> 25.3 us  [the longest x3 23.5 us: kernel_image(): pl.pallas_call(functools.partial(image_kernel, groups, sets, tile_i, tile...]
    ppermute x3, starting transfers between devices: 4.52 us -> 5.65 us  [local(): lax.ppermute(scaled, 'x', [(i, (i - step) % line) for i in range(line)])]
  transfers between devices with their start and end apart: 10 -> 11, of which waited for: 7 -> 4; matrix products, arithmetic and copies ran while one was open for 0% -> 0% of each run, Pallas kernels for 7% -> 20%
where the time goes in v4:
time: 83.6 us; the launch traced here: 83.2 us
  Pallas kernels  27.3 us (33%)
  starting transfers between devices  25.3 us (30%)
  blocking collectives  20.2 us (24%)
  waiting for transfers between devices  5.82 us (7%)
  local copies, waits for them, and re-layouts  2.19 us (3%)
  between operations  1.45 us (2%)
  other arithmetic  0.96 us (1%)
    pallas_call x3, Pallas kernels, kernel_image(): pl.pallas_call(functools.partial(image_kernel, groups, sets, tile_i, tile...  23.5 us
    all_to_all x1, blocking collectives, local(): sums = lax.all_to_all(sums, BLK, 0, 0, tiled=True)  20.2 us
    all_to_all x1, starting transfers between devices, local(): packets = lax.all_to_all(packets, ('yl', *FAR), 0, 0, tiled=True)  9.94 us
    ppermute x3, starting transfers between devices, local(): lax.ppermute(scaled, 'x', [(i, (i - step) % line) for i in range(line)])  5.65 us
    ppermute x3, starting transfers between devices, send(): lax.ppermute(value, 'x', [(i, (i + step) % line) for i in range(line)])  5.5 us
    ppermute x3, waiting for transfers between devices, local(): lax.ppermute(scaled, 'x', [(i, (i - step) % line) for i in range(line)])  2.83 us
    ppermute x1, starting transfers between devices, local(): distant = col_features(place, lax.ppermute(packets, 'yh', swap))  2.38 us
    unnamed x14, local copies, waits for them, and re-layouts  2.19 us
  transfers between devices with their start and end apart: 11, of which 4 were waited for; matrix products, arithmetic and copies ran while one was open for 0% of the time, Pallas kernels for 20%

profile of v4, /device:TPU:8, one launch (start us, length us, event | category | flops | bytes accessed | tf_op | source)
XLA Modules:
  0.0 83.2 jit_solution(933656122920205469)
XLA Ops:
  0.6 0.1 collective-permute-start
  0.7 0.0 copy-start.6
  0.7 0.1 pad_add_fusion.place_ref
  0.8 0.6 copy-done.6
  1.4 0.0 copy-start
  1.4 0.8 copy-done
  2.2 0.0 copy-start.3
  2.2 0.8 %copy-done.3 = f32[16,1024]{1,0:T(8,128)S(1)} copy-done((f32[16,1024]{1,0:T(8,128)S(1)}, f32[16,1024]{1,0:T(8,128)}, u32[]{:S(2)}) %copy-start.3) | copy-done | bytes 65560
  3.0 0.6 prepare.1
  3.6 0.0 collective-permute-done.other_ref
  3.6 1.2 %pack.1 = bf16[16,8,768]{2,1,0:T(8,128)(2,1)} custom-call(s32[2]{0:T(128)S(1)} %pad_add_fusion.place_ref, f32[16,1024]{1,0:T(8,128)S(1)} %get-tuple-element.31.scaled_ref.refs_0_, bf16[8,1024]{1,0:T(8,128)(2,1)S(1)} %get-tuple-element.32.low_ref, f32[8,1024]{1,0:T(8,128)S(1)} %collective-permute-done.other_ref), custom_call_target="tpu_custom_call" | custom-call | tf_op jit(solution)/shard_map/pack/pallas_call | solution.py:261
  4.8 9.9 %all-to-all-start = ((bf16[16,8,768]{2,1,0:T(8,128)(2,1)}), bf16[16,8,768]{2,1,0:T(8,128)(2,1)S(1)}, u32[]{:S(2)}, u32[]{:S(2)}) async-start(bf16[16,8,768]{2,1,0:T(8,128)(2,1)} %pack.1), calls=%async_computation | async-start | bytes 393216 | tf_op jit(solution)/shard_map/all_to_all | solution.py:311
  14.7 1.5 %collective-permute-start.3 = (f32[16,1024]{1,0:T(8,128)S(1)}, f32[16,1024]{1,0:T(8,128)S(1)}, u32[]{:S(2)}, u32[]{:S(2)}) collective-permute-start(f32[16,1024]{1,0:T(8,128)S(1)} %get-tuple-element.31.scaled_ref.refs_0_), channel_id=1, source_target_pairs={{0,4},{4,8},{8,12},{12,0},{1,5},{5,9},{9,13},{13,1},{2,6},{6,10},{... | collective-permute-start | bytes 196616 | tf_op jit(solution)/shard_map/ppermute | solution.py:313
  16.2 2.7 %collective-permute-start.2 = (f32[16,1024]{1,0:T(8,128)S(1)}, f32[16,1024]{1,0:T(8,128)S(1)}, u32[]{:S(2)}, u32[]{:S(2)}) collective-permute-start(f32[16,1024]{1,0:T(8,128)S(1)} %get-tuple-element.31.scaled_ref.refs_0_), channel_id=1, source_target_pairs={{0,8},{4,12},{8,0},{12,4},{1,9},{5,13},{9,1},{13,5},{2,10},{6,14},... | collective-permute-start | bytes 196616 | tf_op jit(solution)/shard_map/ppermute | solution.py:313
  19.0 1.4 %collective-permute-start.1 = (f32[16,1024]{1,0:T(8,128)S(1)}, f32[16,1024]{1,0:T(8,128)S(1)}, u32[]{:S(2)}, u32[]{:S(2)}) collective-permute-start(f32[16,1024]{1,0:T(8,128)S(1)} %get-tuple-element.31.scaled_ref.refs_0_), channel_id=1, source_target_pairs={{0,12},{4,0},{8,4},{12,8},{1,13},{5,1},{9,5},{13,9},{2,14},{6,2},{... | collective-permute-start | bytes 196616 | tf_op jit(solution)/shard_map/ppermute | solution.py:313
  20.4 0.0 collective-permute-done.3.refs_3_
  20.4 1.9 %collective-permute-done.2.refs_2_ = f32[16,1024]{1,0:T(8,128)S(1)} collective-permute-done((f32[16,1024]{1,0:T(8,128)S(1)}, f32[16,1024]{1,0:T(8,128)S(1)}, u32[]{:S(2)}, u32[]{:S(2)}) %collective-permute-start.2) | collective-permute-done | bytes 65568 | tf_op jit(solution)/shard_map/ppermute | solution.py:313
  22.3 1.0 %collective-permute-done.1.refs_1_ = f32[16,1024]{1,0:T(8,128)S(1)} collective-permute-done((f32[16,1024]{1,0:T(8,128)S(1)}, f32[16,1024]{1,0:T(8,128)S(1)}, u32[]{:S(2)}, u32[]{:S(2)}) %collective-permute-start.1) | collective-permute-done | bytes 65568 | tf_op jit(solution)/shard_map/ppermute | solution.py:313
  23.2 0.2 row_features.1
  23.4 0.0 all-to-all-done.packets_ref
  23.4 2.4 %collective-permute-start.4 = (bf16[16,8,768]{2,1,0:T(8,128)(2,1)S(1)}, bf16[16,8,768]{2,1,0:T(8,128)(2,1)S(1)}, u32[]{:S(2)}, u32[]{:S(2)}) collective-permute-start(bf16[16,8,768]{2,1,0:T(8,128)(2,1)S(1)} %all-to-all-done.packets_ref), channel_id=1, source_target_pairs={{0,16},{16,0},{1,17},{17,1},{2,18},{18,2},{3,19},{19,3},{4,20},{20... | collective-permute-start | bytes 589832 | tf_op jit(solution)/shard_map/ppermute | solution.py:324
  25.8 0.8 %col_features.2 = (bf16[2048,64]{1,0:T(8,128)(2,1)S(1)}, bf16[32,2048]{1,0:T(8,128)(2,1)S(1)}) custom-call(s32[2]{0:T(128)S(1)} %pad_add_fusion.place_ref, bf16[16,8,768]{2,1,0:T(8,128)(2,1)S(1)} %all-to-all-done.packets_ref), custom_call_target="tpu_custom_call" | custom-call | tf_op jit(solution)/shard_map/col_features/pallas_call | solution.py:90
  26.6 8.7 %kernel_image.4 = (f32[32,1024]{1,0:T(8,128)S(1)}, f32[32,1024]{1,0:T(8,128)S(1)}, f32[32,1024]{1,0:T(8,128)S(1)}) custom-call(bf16[64,1024]{1,0:T(8,128)(2,1)S(1)} %get-tuple-element.43.refs_0_, bf16[64,1024]{1,0:T(8,128)(2,1)S(1)} %get-tuple-element.44.refs_1_, bf16[64,1024]{1,0:T(8,128)(2,1)S(1)} %get-tuple-element.45.refs_2_, ...), custom_call_target="tpu_custom_call" | custom-call | flops 1207959552 | bytes 4194304 | tf_op jit(solution)/shard_map/kernel_image/pallas_call | solution.py:174
  35.3 0.0 collective-permute-done.4.packets_ref
  35.4 0.8 %col_features.3 = (bf16[2048,64]{1,0:T(8,128)(2,1)S(1)}, bf16[32,2048]{1,0:T(8,128)(2,1)S(1)}) custom-call(s32[2]{0:T(128)S(1)} %pad_add_fusion.place_ref, bf16[16,8,768]{2,1,0:T(8,128)(2,1)S(1)} %collective-permute-done.4.packets_ref), custom_call_target="tpu_custom_call" | custom-call | tf_op jit(solution)/shard_map/col_features/pallas_call | solution.py:90
  36.2 8.7 %kernel_image.5 = (f32[32,1024]{1,0:T(8,128)S(1)}, f32[32,1024]{1,0:T(8,128)S(1)}, f32[32,1024]{1,0:T(8,128)S(1)}) custom-call(bf16[64,1024]{1,0:T(8,128)(2,1)S(1)} %get-tuple-element.43.refs_0_, bf16[64,1024]{1,0:T(8,128)(2,1)S(1)} %get-tuple-element.44.refs_1_, bf16[64,1024]{1,0:T(8,128)(2,1)S(1)} %get-tuple-element.45.refs_2_, ...), custom_call_target="tpu_custom_call" | custom-call | flops 1207959552 | bytes 4194304 | tf_op jit(solution)/shard_map/kernel_image/pallas_call | solution.py:174
  44.9 1.3 %collective-permute-start.5 = (f32[32,1024]{1,0:T(8,128)S(1)}, f32[32,1024]{1,0:T(8,128)S(1)}, u32[]{:S(2)}, u32[]{:S(2)}) collective-permute-start(f32[32,1024]{1,0:T(8,128)S(1)} %get-tuple-element.49), channel_id=1, source_target_pairs={{0,4},{4,8},{8,12},{12,0},{1,5},{5,9},{9,13},{13,1},{2,6},{6,10},{... | collective-permute-start | bytes 393224 | tf_op jit(solution)/shard_map/ppermute | solution.py:319
  46.2 2.9 %collective-permute-start.6 = (f32[32,1024]{1,0:T(8,128)S(1)}, f32[32,1024]{1,0:T(8,128)S(1)}, u32[]{:S(2)}, u32[]{:S(2)}) collective-permute-start(f32[32,1024]{1,0:T(8,128)S(1)} %get-tuple-element.50), channel_id=1, source_target_pairs={{0,8},{4,12},{8,0},{12,4},{1,9},{5,13},{9,1},{13,5},{2,10},{6,14},... | collective-permute-start | bytes 393224 | tf_op jit(solution)/shard_map/ppermute | solution.py:319
  49.1 1.3 %collective-permute-start.7 = (f32[32,1024]{1,0:T(8,128)S(1)}, f32[32,1024]{1,0:T(8,128)S(1)}, u32[]{:S(2)}, u32[]{:S(2)}) collective-permute-start(f32[32,1024]{1,0:T(8,128)S(1)} %get-tuple-element.51), channel_id=1, source_target_pairs={{0,12},{4,0},{8,4},{12,8},{1,13},{5,1},{9,5},{13,9},{2,14},{6,2},{... | collective-permute-start | bytes 393224 | tf_op jit(solution)/shard_map/ppermute | solution.py:319
  50.4 6.1 %kernel_image.3.refs_0_ = f32[32,1024]{1,0:T(8,128)S(1)} custom-call(bf16[64,1024]{1,0:T(8,128)(2,1)S(1)} %get-tuple-element.37.refs_0_, bf16[2048,64]{1,0:T(8,128)(2,1)S(1)} %get-tuple-element.39.refs_1_.refs_3_, bf16[2048,64]{1,0:T(8,128)(2,1)S(1)} %get-tuple-element.40.refs_2_.refs_3_, bf16[32,2048]{1,0:T(8,128)(2,1)S(1)} %get-tuple-element.41.refs_3_.refs_4_, ...), custom_call_target="tpu_custom_call" | custom-call | flops 805306368 | bytes 4194304 | tf_op jit(solution)/shard_map/kernel_image/pallas_call | solution.py:174
  56.5 0.0 collective-permute-done.5.refs_1_
  56.5 0.0 collective-permute-done.6.refs_2_
  56.5 0.0 collective-permute-done.7.refs_3_
  56.6 0.1 collective-permute-start.8
  56.7 1.2 %collective-permute-done.8.refs_1_ = f32[16,1024]{1,0:T(8,128)S(1)} collective-permute-done((f32[16,1024]{1,0:T(8,128)S(1)}, f32[16,1024]{1,0:T(8,128)S(1)}, u32[]{:S(2)}, u32[]{:S(2)}) %collective-permute-start.8) | collective-permute-done | bytes 65568 | tf_op jit(solution)/shard_map/ppermute | solution.py:329
  57.9 0.0 copy-start.1
  57.9 0.0 copy-start.2
  57.9 0.0 copy-start.4
  57.9 0.0 copy-start.5
  57.9 1.6 %collective-permute-start.9 = (f32[8,1024]{1,0:T(8,128)S(1)}, f32[8,1024]{1,0:T(8,128)S(1)}, u32[]{:S(2)}, u32[]{:S(2)}) collective-permute-start(f32[8,1024]{1,0:T(8,128)S(1)} %get-tuple-element.55), channel_id=1, source_target_pairs={{0,2},{2,0},{1,3},{3,1},{4,6},{6,4},{5,7},{7,5},{8,10},{10,8},{9,1... | collective-permute-start | bytes 98312 | tf_op jit(solution)/shard_map/ppermute | solution.py:330
  60.2 1.7 %collective-permute-done.9.refs_1_ = f32[8,1024]{1,0:T(8,128)S(1)} collective-permute-done((f32[8,1024]{1,0:T(8,128)S(1)}, f32[8,1024]{1,0:T(8,128)S(1)}, u32[]{:S(2)}, u32[]{:S(2)}) %collective-permute-start.9) | collective-permute-done | bytes 32800 | tf_op jit(solution)/shard_map/ppermute | solution.py:330
  62.0 0.0 copy-done.1
  62.0 0.0 copy-done.2
  62.0 0.0 copy-done.4
  62.0 0.0 copy-done.5
  62.0 0.1 column_sums.1
  62.1 20.2 %all_to_all.14 = f32[64,1,128]{2,1,0:T(1,128)S(1)} all-to-all(f32[64,1,128]{2,1,0:T(1,128)S(1)} %bitcast.6), channel_id=1, replica_groups=mesh['z'=8,'yh'=2,'x'=4,'yl'=2,'core'=2] {'z','yh','x'}, dimensions={0} | all-to-all | bytes 65536 | tf_op jit(solution)/shard_map/all_to_all | solution.py:334
  82.3 0.1 reduce_sum.9
  82.4 0.1 maximum_divide_fusion
  82.5 0.7 multiply_add_fusion
  (2 shorter events, 0.0 us)
Async XLA Ops:
  0.6 2.9 %collective-permute-start = (f32[8,1024]{1,0:T(8,128)}, f32[8,1024]{1,0:T(8,128)S(1)}, u32[]{:S(2)}, u32[]{:S(2)}) collective-permute-start(f32[8,1024]{1,0:T(8,128)} %direction_ref.3), channel_id=1, source_target_pairs={{0,1},{1,0},{2,3},{3,2},{4,5},{5,4},{6,7},{7,6},{8,9},{9,8},{10,11... | collective-permute-start | bytes 98312 | tf_op jit(solution)/shard_map/ppermute | solution.py:308
  0.7 0.7 copy-start.6
  1.4 0.8 copy-start
  2.2 0.8 %copy-start.3 = (f32[16,1024]{1,0:T(8,128)S(1)}, f32[16,1024]{1,0:T(8,128)}, u32[]{:S(2)}) copy-start(f32[16,1024]{1,0:T(8,128)} %points_ref.1) | copy-start | bytes 196612
  4.8 18.6 %all-to-all-start = ((bf16[16,8,768]{2,1,0:T(8,128)(2,1)}), bf16[16,8,768]{2,1,0:T(8,128)(2,1)S(1)}, u32[]{:S(2)}, u32[]{:S(2)}) async-start(bf16[16,8,768]{2,1,0:T(8,128)(2,1)} %pack.1), calls=%async_computation | async-start | bytes 393216 | tf_op jit(solution)/shard_map/all_to_all | solution.py:311
  14.7 5.7 %collective-permute-start.3 = (f32[16,1024]{1,0:T(8,128)S(1)}, f32[16,1024]{1,0:T(8,128)S(1)}, u32[]{:S(2)}, u32[]{:S(2)}) collective-permute-start(f32[16,1024]{1,0:T(8,128)S(1)} %get-tuple-element.31.scaled_ref.refs_0_), channel_id=1, source_target_pairs={{0,4},{4,8},{8,12},{12,0},{1,5},{5,9},{9,13},{13,1},{2,6},{6,10},{... | collective-permute-start | bytes 196616 | tf_op jit(solution)/shard_map/ppermute | solution.py:313
  16.2 6.0 %collective-permute-start.2 = (f32[16,1024]{1,0:T(8,128)S(1)}, f32[16,1024]{1,0:T(8,128)S(1)}, u32[]{:S(2)}, u32[]{:S(2)}) collective-permute-start(f32[16,1024]{1,0:T(8,128)S(1)} %get-tuple-element.31.scaled_ref.refs_0_), channel_id=1, source_target_pairs={{0,8},{4,12},{8,0},{12,4},{1,9},{5,13},{9,1},{13,5},{2,10},{6,14},... | collective-permute-start | bytes 196616 | tf_op jit(solution)/shard_map/ppermute | solution.py:313
  19.0 4.3 %collective-permute-start.1 = (f32[16,1024]{1,0:T(8,128)S(1)}, f32[16,1024]{1,0:T(8,128)S(1)}, u32[]{:S(2)}, u32[]{:S(2)}) collective-permute-start(f32[16,1024]{1,0:T(8,128)S(1)} %get-tuple-element.31.scaled_ref.refs_0_), channel_id=1, source_target_pairs={{0,12},{4,0},{8,4},{12,8},{1,13},{5,1},{9,5},{13,9},{2,14},{6,2},{... | collective-permute-start | bytes 196616 | tf_op jit(solution)/shard_map/ppermute | solution.py:313
  23.4 11.9 %collective-permute-start.4 = (bf16[16,8,768]{2,1,0:T(8,128)(2,1)S(1)}, bf16[16,8,768]{2,1,0:T(8,128)(2,1)S(1)}, u32[]{:S(2)}, u32[]{:S(2)}) collective-permute-start(bf16[16,8,768]{2,1,0:T(8,128)(2,1)S(1)} %all-to-all-done.packets_ref), channel_id=1, source_target_pairs={{0,16},{16,0},{1,17},{17,1},{2,18},{18,2},{3,19},{19,3},{4,20},{20... | collective-permute-start | bytes 589832 | tf_op jit(solution)/shard_map/ppermute | solution.py:324
  44.9 11.6 %collective-permute-start.5 = (f32[32,1024]{1,0:T(8,128)S(1)}, f32[32,1024]{1,0:T(8,128)S(1)}, u32[]{:S(2)}, u32[]{:S(2)}) collective-permute-start(f32[32,1024]{1,0:T(8,128)S(1)} %get-tuple-element.49), channel_id=1, source_target_pairs={{0,4},{4,8},{8,12},{12,0},{1,5},{5,9},{9,13},{13,1},{2,6},{6,10},{... | collective-permute-start | bytes 393224 | tf_op jit(solution)/shard_map/ppermute | solution.py:319
  46.2 10.3 %collective-permute-start.6 = (f32[32,1024]{1,0:T(8,128)S(1)}, f32[32,1024]{1,0:T(8,128)S(1)}, u32[]{:S(2)}, u32[]{:S(2)}) collective-permute-start(f32[32,1024]{1,0:T(8,128)S(1)} %get-tuple-element.50), channel_id=1, source_target_pairs={{0,8},{4,12},{8,0},{12,4},{1,9},{5,13},{9,1},{13,5},{2,10},{6,14},... | collective-permute-start | bytes 393224 | tf_op jit(solution)/shard_map/ppermute | solution.py:319
  49.1 7.4 %collective-permute-start.7 = (f32[32,1024]{1,0:T(8,128)S(1)}, f32[32,1024]{1,0:T(8,128)S(1)}, u32[]{:S(2)}, u32[]{:S(2)}) collective-permute-start(f32[32,1024]{1,0:T(8,128)S(1)} %get-tuple-element.51), channel_id=1, source_target_pairs={{0,12},{4,0},{8,4},{12,8},{1,13},{5,1},{9,5},{13,9},{2,14},{6,2},{... | collective-permute-start | bytes 393224 | tf_op jit(solution)/shard_map/ppermute | solution.py:319
  56.6 1.3 %collective-permute-start.8 = (f32[16,1024]{1,0:T(8,128)S(1)}, f32[16,1024]{1,0:T(8,128)S(1)}, u32[]{:S(2)}, u32[]{:S(2)}) collective-permute-start(f32[16,1024]{1,0:T(8,128)S(1)} %get-tuple-element.53), channel_id=1, source_target_pairs={{0,1},{1,0},{2,3},{3,2},{4,5},{5,4},{6,7},{7,6},{8,9},{9,8},{10,11... | collective-permute-start | bytes 196616 | tf_op jit(solution)/shard_map/ppermute | solution.py:329
  57.9 4.0 %copy-start.1 = (f32[8,1024]{1,0:T(8,128)S(1)}, f32[8,1024]{1,0:T(8,128)}, u32[]{:S(2)}) copy-start(f32[8,1024]{1,0:T(8,128)} %direction_ref.3) | copy-start | bytes 98308
  57.9 4.0 %copy-start.2 = (f32[8,1024]{1,0:T(8,128)S(1)}, f32[8,1024]{1,0:T(8,128)}, u32[]{:S(2)}) copy-start(f32[8,1024]{1,0:T(8,128)} %residual_ref.1) | copy-start | bytes 98308
  57.9 4.0 %copy-start.4 = (f32[8,1024]{1,0:T(8,128)S(1)}, f32[8,1024]{1,0:T(8,128)}, u32[]{:S(2)}) copy-start(f32[8,1024]{1,0:T(8,128)} %solution_ref.1) | copy-start | bytes 98308
  57.9 4.0 %copy-start.5 = (f32[1024]{0:T(1024)S(1)}, f32[1024]{0:T(1024)}, u32[]{:S(2)}) copy-start(f32[1024]{0:T(1024)} %param.9) | copy-start | bytes 12292
  57.9 4.0 %collective-permute-start.9 = (f32[8,1024]{1,0:T(8,128)S(1)}, f32[8,1024]{1,0:T(8,128)S(1)}, u32[]{:S(2)}, u32[]{:S(2)}) collective-permute-start(f32[8,1024]{1,0:T(8,128)S(1)} %get-tuple-element.55), channel_id=1, source_target_pairs={{0,2},{2,0},{1,3},{3,1},{4,6},{6,4},{5,7},{7,5},{8,10},{10,8},{9,1... | collective-permute-start | bytes 98312 | tf_op jit(solution)/shard_map/ppermute | solution.py:330

commit v5 on v4

--- a/solution.py
+++ b/solution.py
@@ -70,18 +70,14 @@
         one = jnp.ones((1, piece), F32)
         misc = stack_rows((one, one, one, *norm), piece)
         cross = -2.0 * value
-        place = pl.ds(pl.multiple_of(p * piece, piece), piece)
+        place = slice(p * piece, (p + 1) * piece)
         col_f[place, :] = jnp.concatenate([cross, cross, cross, misc], axis=0).T.astype(BF16)
         parts = [packets_ref[q * pieces + p].astype(F32) for q in (yl, 1 - yl)]
         columns = [part[:, k * piece : (k + 1) * piece] for k in range(2) for part in parts]
         low[:, place] = jnp.concatenate(columns, axis=0).astype(BF16)
 
-    def some(index, _):
-        for k in range(4):
-            features(4 * index + k)
-        return 0
-
-    lax.fori_loop(0, pieces // 4, some, 0)
+    for p in range(pieces):
+        features(p)
 
 
 def col_features(place, packets):
@@ -105,11 +101,17 @@
     part_j, count_j = low_refs[0].shape[1], low.shape[1]
     width = out_refs[0].shape[1]
     count_i = groups * width
-    for g in range(groups):
-        rows[:, g * width : (g + 1) * width] = rows_refs[g][...]
-    for k in range(sets):
-        col_f[k * part_j : (k + 1) * part_j, :] = col_refs[k][...]
-        low[:, k * part_j : (k + 1) * part_j] = low_refs[k][...]
+    if groups == 1:
+        rows = rows_refs[0]
+    else:
+        for g in range(groups):
+            rows[:, g * width : (g + 1) * width] = rows_refs[g][...]
+    if sets == 1:
+        col_f, low = col_refs[0], low_refs[0]
+    else:
+        for k in range(sets):
+            col_f[k * part_j : (k + 1) * part_j, :] = col_refs[k][...]
+            low[:, k * part_j : (k + 1) * part_j] = low_refs[k][...]
     per = count_j // tile_j
     steps = (count_i // tile_i) * per
     per_group = width // tile_i
@@ -310,13 +312,13 @@
     packets = pack(far, place, scaled, low, other)
     packets = lax.all_to_all(packets, ("yl", *FAR), 0, 0, tiled=True)
     blocks = [scaled] + [
-        lax.ppermute(scaled, "x", [(i, (i - step) % line) for i in range(line)])
+        lax.ppermute(scaled, "x", [(i, i ^ step) for i in range(line)])
         for step in range(1, line)
     ]
     rows = row_features(blocks)
 
     def send(value, step):
-        return lax.ppermute(value, "x", [(i, (i + step) % line) for i in range(line)])
+        return lax.ppermute(value, "x", [(i, i ^ step) for i in range(line)])
 
     packets, *rows = lax.optimization_barrier((packets, *rows))
     near = col_features(place, packets)

time: 83.6 us -> 83.3 us (level)
  starting transfers between devices: 25.3 us -> 22.7 us
  waiting for transfers between devices: 5.82 us -> 7.86 us
    ppermute x6, starting transfers between devices: 11.2 us -> 8.88 us  [the longest x3 4.79 us: send(): return lax.ppermute(value, 'x', [(i, i ^ step) for i in range(line)])]
    ppermute x6, waiting for transfers between devices: 2.84 us -> 4.53 us  [the longest x3 4.52 us: local(): lax.ppermute(scaled, 'x', [(i, i ^ step) for i in range(line)])]
where the time goes in v5:
time: 83.3 us; the launch traced here: 82.9 us
  Pallas kernels  27 us (32%)
  starting transfers between devices  22.7 us (27%)
  blocking collectives  20.8 us (25%)
  waiting for transfers between devices  7.86 us (9%)
  local copies, waits for them, and re-layouts  2.19 us (3%)
  between operations  1.45 us (2%)
  other arithmetic  0.96 us (1%)
    pallas_call x3, Pallas kernels, kernel_image(): pl.pallas_call(functools.partial(image_kernel, groups, sets, tile_i, tile...  23.4 us
    all_to_all x1, blocking collectives, local(): sums = lax.all_to_all(sums, BLK, 0, 0, tiled=True)  20.8 us
    all_to_all x1, starting transfers between devices, local(): packets = lax.all_to_all(packets, ('yl', *FAR), 0, 0, tiled=True)  9.94 us
    ppermute x3, starting transfers between devices, send(): return lax.ppermute(value, 'x', [(i, i ^ step) for i in range(line)])  4.79 us
    ppermute x3, waiting for transfers between devices, local(): lax.ppermute(scaled, 'x', [(i, i ^ step) for i in range(line)])  4.52 us
    ppermute x3, starting transfers between devices, local(): lax.ppermute(scaled, 'x', [(i, i ^ step) for i in range(line)])  4.09 us
    ppermute x1, starting transfers between devices, local(): distant = col_features(place, lax.ppermute(packets, 'yh', swap))  2.38 us
    unnamed x14, local copies, waits for them, and re-layouts  2.19 us
  transfers between devices with their start and end apart: 11, of which 4 were waited for; matrix products, arithmetic and copies ran while one was open for 0% of the time, Pallas kernels for 20%

profile of v5, /device:TPU:8, one launch (start us, length us, event | category | flops | bytes accessed | tf_op | source)
XLA Modules:
  0.0 82.9 jit_solution(2843369431680064922)
XLA Ops:
  0.6 0.1 collective-permute-start
  0.7 0.0 copy-start.6
  0.7 0.1 pad_add_fusion.place_ref
  0.8 0.6 copy-done.6
  1.4 0.0 copy-start
  1.4 0.8 copy-done
  2.2 0.0 copy-start.3
  2.2 0.8 %copy-done.3 = f32[16,1024]{1,0:T(8,128)S(1)} copy-done((f32[16,1024]{1,0:T(8,128)S(1)}, f32[16,1024]{1,0:T(8,128)}, u32[]{:S(2)}) %copy-start.3) | copy-done | bytes 65560
  3.0 0.6 prepare.1
  3.6 0.0 collective-permute-done.other_ref
  3.6 1.2 %pack.1 = bf16[16,8,768]{2,1,0:T(8,128)(2,1)} custom-call(s32[2]{0:T(128)S(1)} %pad_add_fusion.place_ref, f32[16,1024]{1,0:T(8,128)S(1)} %get-tuple-element.31.scaled_ref.refs_0_, bf16[8,1024]{1,0:T(8,128)(2,1)S(1)} %get-tuple-element.32.low_ref, f32[8,1024]{1,0:T(8,128)S(1)} %collective-permute-done.other_ref), custom_call_target="tpu_custom_call" | custom-call | tf_op jit(solution)/shard_map/pack/pallas_call | solution.py:263
  4.8 9.9 %all-to-all-start = ((bf16[16,8,768]{2,1,0:T(8,128)(2,1)}), bf16[16,8,768]{2,1,0:T(8,128)(2,1)S(1)}, u32[]{:S(2)}, u32[]{:S(2)}) async-start(bf16[16,8,768]{2,1,0:T(8,128)(2,1)} %pack.1), calls=%async_computation | async-start | bytes 393216 | tf_op jit(solution)/shard_map/all_to_all | solution.py:313
  14.7 2.8 %collective-permute-start.3 = (f32[16,1024]{1,0:T(8,128)S(1)}, f32[16,1024]{1,0:T(8,128)S(1)}, u32[]{:S(2)}, u32[]{:S(2)}) collective-permute-start(f32[16,1024]{1,0:T(8,128)S(1)} %get-tuple-element.31.scaled_ref.refs_0_), channel_id=1, source_target_pairs={{0,12},{4,8},{8,4},{12,0},{1,13},{5,9},{9,5},{13,1},{2,14},{6,10},... | collective-permute-start | bytes 196616 | tf_op jit(solution)/shard_map/ppermute | solution.py:315
  17.5 0.8 collective-permute-start.2
  18.3 0.5 collective-permute-start.1
  18.8 1.4 %collective-permute-done.3.refs_3_ = f32[16,1024]{1,0:T(8,128)S(1)} collective-permute-done((f32[16,1024]{1,0:T(8,128)S(1)}, f32[16,1024]{1,0:T(8,128)S(1)}, u32[]{:S(2)}, u32[]{:S(2)}) %collective-permute-start.3) | collective-permute-done | bytes 65568 | tf_op jit(solution)/shard_map/ppermute | solution.py:315
  20.2 3.1 %collective-permute-done.2.refs_2_ = f32[16,1024]{1,0:T(8,128)S(1)} collective-permute-done((f32[16,1024]{1,0:T(8,128)S(1)}, f32[16,1024]{1,0:T(8,128)S(1)}, u32[]{:S(2)}, u32[]{:S(2)}) %collective-permute-start.2) | collective-permute-done | bytes 65568 | tf_op jit(solution)/shard_map/ppermute | solution.py:315
  23.4 0.0 collective-permute-done.1.refs_1_
  23.4 0.2 row_features.1
  23.5 0.0 all-to-all-done.packets_ref
  23.5 2.4 %collective-permute-start.4 = (bf16[16,8,768]{2,1,0:T(8,128)(2,1)S(1)}, bf16[16,8,768]{2,1,0:T(8,128)(2,1)S(1)}, u32[]{:S(2)}, u32[]{:S(2)}) collective-permute-start(bf16[16,8,768]{2,1,0:T(8,128)(2,1)S(1)} %all-to-all-done.packets_ref), channel_id=1, source_target_pairs={{0,16},{16,0},{1,17},{17,1},{2,18},{18,2},{3,19},{19,3},{4,20},{20... | collective-permute-start | bytes 589832 | tf_op jit(solution)/shard_map/ppermute | solution.py:326
  25.9 0.8 col_features.2
  26.7 8.7 %kernel_image.4 = (f32[32,1024]{1,0:T(8,128)S(1)}, f32[32,1024]{1,0:T(8,128)S(1)}, f32[32,1024]{1,0:T(8,128)S(1)}) custom-call(bf16[64,1024]{1,0:T(8,128)(2,1)S(1)} %get-tuple-element.43.refs_0_, bf16[64,1024]{1,0:T(8,128)(2,1)S(1)} %get-tuple-element.44.refs_1_, bf16[64,1024]{1,0:T(8,128)(2,1)S(1)} %get-tuple-element.45.refs_2_, ...), custom_call_target="tpu_custom_call" | custom-call | flops 1207959552 | bytes 4194304 | tf_op jit(solution)/shard_map/kernel_image/pallas_call | solution.py:176
  35.3 0.0 collective-permute-done.4.packets_ref
  35.4 0.8 col_features.3
  36.1 8.7 %kernel_image.5 = (f32[32,1024]{1,0:T(8,128)S(1)}, f32[32,1024]{1,0:T(8,128)S(1)}, f32[32,1024]{1,0:T(8,128)S(1)}) custom-call(bf16[64,1024]{1,0:T(8,128)(2,1)S(1)} %get-tuple-element.43.refs_0_, bf16[64,1024]{1,0:T(8,128)(2,1)S(1)} %get-tuple-element.44.refs_1_, bf16[64,1024]{1,0:T(8,128)(2,1)S(1)} %get-tuple-element.45.refs_2_, ...), custom_call_target="tpu_custom_call" | custom-call | flops 1207959552 | bytes 4194304 | tf_op jit(solution)/shard_map/kernel_image/pallas_call | solution.py:176
  44.8 1.2 %collective-permute-start.5 = (f32[32,1024]{1,0:T(8,128)S(1)}, f32[32,1024]{1,0:T(8,128)S(1)}, u32[]{:S(2)}, u32[]{:S(2)}) collective-permute-start(f32[32,1024]{1,0:T(8,128)S(1)} %get-tuple-element.49), channel_id=1, source_target_pairs={{0,4},{4,0},{8,12},{12,8},{1,5},{5,1},{9,13},{13,9},{2,6},{6,2},{1... | collective-permute-start | bytes 393224 | tf_op jit(solution)/shard_map/ppermute | solution.py:321
  46.0 2.7 %collective-permute-start.6 = (f32[32,1024]{1,0:T(8,128)S(1)}, f32[32,1024]{1,0:T(8,128)S(1)}, u32[]{:S(2)}, u32[]{:S(2)}) collective-permute-start(f32[32,1024]{1,0:T(8,128)S(1)} %get-tuple-element.50), channel_id=1, source_target_pairs={{0,8},{4,12},{8,0},{12,4},{1,9},{5,13},{9,1},{13,5},{2,10},{6,14},... | collective-permute-start | bytes 393224 | tf_op jit(solution)/shard_map/ppermute | solution.py:321
  48.7 0.8 %collective-permute-start.7 = (f32[32,1024]{1,0:T(8,128)S(1)}, f32[32,1024]{1,0:T(8,128)S(1)}, u32[]{:S(2)}, u32[]{:S(2)}) collective-permute-start(f32[32,1024]{1,0:T(8,128)S(1)} %get-tuple-element.51), channel_id=1, source_target_pairs={{0,12},{4,8},{8,4},{12,0},{1,13},{5,9},{9,5},{13,1},{2,14},{6,10},... | collective-permute-start | bytes 393224 | tf_op jit(solution)/shard_map/ppermute | solution.py:321
  49.6 6.1 %kernel_image.3.refs_0_ = f32[32,1024]{1,0:T(8,128)S(1)} custom-call(bf16[64,1024]{1,0:T(8,128)(2,1)S(1)} %get-tuple-element.37.refs_0_, bf16[2048,64]{1,0:T(8,128)(2,1)S(1)} %get-tuple-element.39.refs_1_.refs_3_, bf16[2048,64]{1,0:T(8,128)(2,1)S(1)} %get-tuple-element.40.refs_2_.refs_3_, bf16[32,2048]{1,0:T(8,128)(2,1)S(1)} %get-tuple-element.41.refs_3_.refs_4_, ...), custom_call_target="tpu_custom_call" | custom-call | flops 805306368 | bytes 4194304 | tf_op jit(solution)/shard_map/kernel_image/pallas_call | solution.py:176
  55.7 0.0 collective-permute-done.5.refs_1_
  55.7 0.0 collective-permute-done.6.refs_2_
  55.7 0.0 collective-permute-done.7.refs_3_
  55.7 0.1 collective-permute-start.8
  55.8 1.2 %collective-permute-done.8.refs_1_ = f32[16,1024]{1,0:T(8,128)S(1)} collective-permute-done((f32[16,1024]{1,0:T(8,128)S(1)}, f32[16,1024]{1,0:T(8,128)S(1)}, u32[]{:S(2)}, u32[]{:S(2)}) %collective-permute-start.8) | collective-permute-done | bytes 65568 | tf_op jit(solution)/shard_map/ppermute | solution.py:331
  57.1 0.0 copy-start.1
  57.1 0.0 copy-start.2
  57.1 0.0 copy-start.4
  57.1 0.0 copy-start.5
  57.1 1.3 %collective-permute-start.9 = (f32[8,1024]{1,0:T(8,128)S(1)}, f32[8,1024]{1,0:T(8,128)S(1)}, u32[]{:S(2)}, u32[]{:S(2)}) collective-permute-start(f32[8,1024]{1,0:T(8,128)S(1)} %get-tuple-element.55), channel_id=1, source_target_pairs={{0,2},{2,0},{1,3},{3,1},{4,6},{6,4},{5,7},{7,5},{8,10},{10,8},{9,1... | collective-permute-start | bytes 98312 | tf_op jit(solution)/shard_map/ppermute | solution.py:332
  59.0 2.1 %collective-permute-done.9.refs_1_ = f32[8,1024]{1,0:T(8,128)S(1)} collective-permute-done((f32[8,1024]{1,0:T(8,128)S(1)}, f32[8,1024]{1,0:T(8,128)S(1)}, u32[]{:S(2)}, u32[]{:S(2)}) %collective-permute-start.9) | collective-permute-done | bytes 32800 | tf_op jit(solution)/shard_map/ppermute | solution.py:332
  61.1 0.0 copy-done.1
  61.1 0.0 copy-done.2
  61.1 0.0 copy-done.4
  61.1 0.0 copy-done.5
  61.1 0.1 column_sums.1
  61.2 20.8 %all_to_all.14 = f32[64,1,128]{2,1,0:T(1,128)S(1)} all-to-all(f32[64,1,128]{2,1,0:T(1,128)S(1)} %bitcast.6), channel_id=1, replica_groups=mesh['z'=8,'yh'=2,'x'=4,'yl'=2,'core'=2] {'z','yh','x'}, dimensions={0} | all-to-all | bytes 65536 | tf_op jit(solution)/shard_map/all_to_all | solution.py:336
  82.0 0.1 reduce_sum.9
  82.1 0.1 maximum_divide_fusion
  82.2 0.7 multiply_add_fusion
  (2 shorter events, 0.0 us)
Async XLA Ops:
  0.6 2.9 %collective-permute-start = (f32[8,1024]{1,0:T(8,128)}, f32[8,1024]{1,0:T(8,128)S(1)}, u32[]{:S(2)}, u32[]{:S(2)}) collective-permute-start(f32[8,1024]{1,0:T(8,128)} %direction_ref.3), channel_id=1, source_target_pairs={{0,1},{1,0},{2,3},{3,2},{4,5},{5,4},{6,7},{7,6},{8,9},{9,8},{10,11... | collective-permute-start | bytes 98312 | tf_op jit(solution)/shard_map/ppermute | solution.py:310
  0.7 0.7 copy-start.6
  1.4 0.8 copy-start
  2.2 0.8 %copy-start.3 = (f32[16,1024]{1,0:T(8,128)S(1)}, f32[16,1024]{1,0:T(8,128)}, u32[]{:S(2)}) copy-start(f32[16,1024]{1,0:T(8,128)} %points_ref.1) | copy-start | bytes 196612
  4.8 18.7 %all-to-all-start = ((bf16[16,8,768]{2,1,0:T(8,128)(2,1)}), bf16[16,8,768]{2,1,0:T(8,128)(2,1)S(1)}, u32[]{:S(2)}, u32[]{:S(2)}) async-start(bf16[16,8,768]{2,1,0:T(8,128)(2,1)} %pack.1), calls=%async_computation | async-start | bytes 393216 | tf_op jit(solution)/shard_map/all_to_all | solution.py:313
  14.7 5.5 %collective-permute-start.3 = (f32[16,1024]{1,0:T(8,128)S(1)}, f32[16,1024]{1,0:T(8,128)S(1)}, u32[]{:S(2)}, u32[]{:S(2)}) collective-permute-start(f32[16,1024]{1,0:T(8,128)S(1)} %get-tuple-element.31.scaled_ref.refs_0_), channel_id=1, source_target_pairs={{0,12},{4,8},{8,4},{12,0},{1,13},{5,9},{9,5},{13,1},{2,14},{6,10},... | collective-permute-start | bytes 196616 | tf_op jit(solution)/shard_map/ppermute | solution.py:315
  17.5 5.9 %collective-permute-start.2 = (f32[16,1024]{1,0:T(8,128)S(1)}, f32[16,1024]{1,0:T(8,128)S(1)}, u32[]{:S(2)}, u32[]{:S(2)}) collective-permute-start(f32[16,1024]{1,0:T(8,128)S(1)} %get-tuple-element.31.scaled_ref.refs_0_), channel_id=1, source_target_pairs={{0,8},{4,12},{8,0},{12,4},{1,9},{5,13},{9,1},{13,5},{2,10},{6,14},... | collective-permute-start | bytes 196616 | tf_op jit(solution)/shard_map/ppermute | solution.py:315
  18.3 5.1 %collective-permute-start.1 = (f32[16,1024]{1,0:T(8,128)S(1)}, f32[16,1024]{1,0:T(8,128)S(1)}, u32[]{:S(2)}, u32[]{:S(2)}) collective-permute-start(f32[16,1024]{1,0:T(8,128)S(1)} %get-tuple-element.31.scaled_ref.refs_0_), channel_id=1, source_target_pairs={{0,4},{4,0},{8,12},{12,8},{1,5},{5,1},{9,13},{13,9},{2,6},{6,2},{1... | collective-permute-start | bytes 196616 | tf_op jit(solution)/shard_map/ppermute | solution.py:315
  23.5 11.8 %collective-permute-start.4 = (bf16[16,8,768]{2,1,0:T(8,128)(2,1)S(1)}, bf16[16,8,768]{2,1,0:T(8,128)(2,1)S(1)}, u32[]{:S(2)}, u32[]{:S(2)}) collective-permute-start(bf16[16,8,768]{2,1,0:T(8,128)(2,1)S(1)} %all-to-all-done.packets_ref), channel_id=1, source_target_pairs={{0,16},{16,0},{1,17},{17,1},{2,18},{18,2},{3,19},{19,3},{4,20},{20... | collective-permute-start | bytes 589832 | tf_op jit(solution)/shard_map/ppermute | solution.py:326
  44.8 10.9 %collective-permute-start.5 = (f32[32,1024]{1,0:T(8,128)S(1)}, f32[32,1024]{1,0:T(8,128)S(1)}, u32[]{:S(2)}, u32[]{:S(2)}) collective-permute-start(f32[32,1024]{1,0:T(8,128)S(1)} %get-tuple-element.49), channel_id=1, source_target_pairs={{0,4},{4,0},{8,12},{12,8},{1,5},{5,1},{9,13},{13,9},{2,6},{6,2},{1... | collective-permute-start | bytes 393224 | tf_op jit(solution)/shard_map/ppermute | solution.py:321
  46.0 9.7 %collective-permute-start.6 = (f32[32,1024]{1,0:T(8,128)S(1)}, f32[32,1024]{1,0:T(8,128)S(1)}, u32[]{:S(2)}, u32[]{:S(2)}) collective-permute-start(f32[32,1024]{1,0:T(8,128)S(1)} %get-tuple-element.50), channel_id=1, source_target_pairs={{0,8},{4,12},{8,0},{12,4},{1,9},{5,13},{9,1},{13,5},{2,10},{6,14},... | collective-permute-start | bytes 393224 | tf_op jit(solution)/shard_map/ppermute | solution.py:321
  48.7 7.0 %collective-permute-start.7 = (f32[32,1024]{1,0:T(8,128)S(1)}, f32[32,1024]{1,0:T(8,128)S(1)}, u32[]{:S(2)}, u32[]{:S(2)}) collective-permute-start(f32[32,1024]{1,0:T(8,128)S(1)} %get-tuple-element.51), channel_id=1, source_target_pairs={{0,12},{4,8},{8,4},{12,0},{1,13},{5,9},{9,5},{13,1},{2,14},{6,10},... | collective-permute-start | bytes 393224 | tf_op jit(solution)/shard_map/ppermute | solution.py:321
  55.7 1.3 %collective-permute-start.8 = (f32[16,1024]{1,0:T(8,128)S(1)}, f32[16,1024]{1,0:T(8,128)S(1)}, u32[]{:S(2)}, u32[]{:S(2)}) collective-permute-start(f32[16,1024]{1,0:T(8,128)S(1)} %get-tuple-element.53), channel_id=1, source_target_pairs={{0,1},{1,0},{2,3},{3,2},{4,5},{5,4},{6,7},{7,6},{8,9},{9,8},{10,11... | collective-permute-start | bytes 196616 | tf_op jit(solution)/shard_map/ppermute | solution.py:331
  57.1 4.0 %copy-start.1 = (f32[8,1024]{1,0:T(8,128)S(1)}, f32[8,1024]{1,0:T(8,128)}, u32[]{:S(2)}) copy-start(f32[8,1024]{1,0:T(8,128)} %direction_ref.3) | copy-start | bytes 98308
  57.1 4.0 %copy-start.2 = (f32[8,1024]{1,0:T(8,128)S(1)}, f32[8,1024]{1,0:T(8,128)}, u32[]{:S(2)}) copy-start(f32[8,1024]{1,0:T(8,128)} %residual_ref.1) | copy-start | bytes 98308
  57.1 4.0 %copy-start.4 = (f32[8,1024]{1,0:T(8,128)S(1)}, f32[8,1024]{1,0:T(8,128)}, u32[]{:S(2)}) copy-start(f32[8,1024]{1,0:T(8,128)} %solution_ref.1) | copy-start | bytes 98308
  57.1 4.0 %copy-start.5 = (f32[1024]{0:T(1024)S(1)}, f32[1024]{0:T(1024)}, u32[]{:S(2)}) copy-start(f32[1024]{0:T(1024)} %param.9) | copy-start | bytes 12292
  57.1 4.0 %collective-permute-start.9 = (f32[8,1024]{1,0:T(8,128)S(1)}, f32[8,1024]{1,0:T(8,128)S(1)}, u32[]{:S(2)}, u32[]{:S(2)}) collective-permute-start(f32[8,1024]{1,0:T(8,128)S(1)} %get-tuple-element.55), channel_id=1, source_target_pairs={{0,2},{2,0},{1,3},{3,1},{4,6},{6,4},{5,7},{7,5},{8,10},{10,8},{9,1... | collective-permute-start | bytes 98312 | tf_op jit(solution)/shard_map/ppermute | solution.py:332

commit v6 on v5

--- a/solution.py
+++ b/solution.py
@@ -36,29 +36,30 @@
     return total
 
 
-def row_kernel(*refs):
+def row_kernel(scale_ref, *refs):
     count = len(refs) // 2
+    scale = scale_ref[:, :1]
     for ref, out_ref in zip(refs[:count], refs[count:]):
-        value = ref[...]
+        value = ref[...] * scale
         norm = split3(jnp.sum(value * value, axis=0, keepdims=True))
         one = jnp.ones((1, value.shape[1]), F32)
         misc = stack_rows((*norm, one, one, one), value.shape[1])
-        out_ref[...] = jnp.concatenate([*split3(value), misc], axis=0).astype(BF16)
-
-
-def row_features(blocks):
+        out_ref[...] = jnp.concatenate([*split3(value * scale), misc], axis=0).astype(BF16)
+
+
+def row_features(scale, blocks):
     vmem = pl.BlockSpec(memory_space=pltpu.VMEM)
     return pl.pallas_call(
         row_kernel,
         out_shape=tuple(jax.ShapeDtypeStruct((64, block.shape[1]), BF16) for block in blocks),
-        in_specs=[vmem] * len(blocks),
+        in_specs=[vmem] * (len(blocks) + 1),
         out_specs=(vmem,) * len(blocks),
         compiler_params=pltpu.CompilerParams(vmem_limit_bytes=8 * 2**20),
         name="row_features",
-    )(*blocks)
-
-
-def col_kernel(place_ref, packets_ref, col_f, low):
+    )(scale, *blocks)
+
+
+def col_kernel(place_ref, scale_ref, packets_ref, col_f, low):
     yl = place_ref[0]
     pieces = packets_ref.shape[0] // 2
     piece = packets_ref.shape[2] // 3
@@ -66,7 +67,8 @@
     def features(p):
         parts = [packets_ref[q * pieces + p].astype(F32) for q in range(2)]
         value = jnp.concatenate([part[:, 2 * piece :] for part in parts], axis=0)
-        norm = split3(jnp.sum(value * value, axis=0, keepdims=True))
+        scaled = value * scale_ref[:, :1]
+        norm = split3(jnp.sum(scaled * scaled, axis=0, keepdims=True))
         one = jnp.ones((1, piece), F32)
         misc = stack_rows((one, one, one, *norm), piece)
         cross = -2.0 * value
@@ -80,17 +82,17 @@
         features(p)
 
 
-def col_features(place, packets):
+def col_features(place, scale, packets):
     vmem = pl.BlockSpec(memory_space=pltpu.VMEM)
     count = packets.shape[0] * packets.shape[2] // 6
     return pl.pallas_call(
         col_kernel,
         out_shape=(jax.ShapeDtypeStruct((count, 64), BF16), jax.ShapeDtypeStruct((32, count), BF16)),
-        in_specs=[pl.BlockSpec(memory_space=pltpu.SMEM), vmem],
+        in_specs=[pl.BlockSpec(memory_space=pltpu.SMEM), vmem, vmem],
         out_specs=(vmem, vmem),
         compiler_params=pltpu.CompilerParams(vmem_limit_bytes=8 * 2**20),
         name="col_features",
-    )(place, packets)
+    )(place, scale, packets)
 
 
 def image_kernel(groups, sets, tile_i, tile_j, more, *refs):
@@ -219,45 +221,38 @@
     )(*parts)
 
 
-def prepare_kernel(lengths_ref, points_ref, direction_ref, scaled_ref, low_ref):
-    dims = points_ref.shape[0]
-    index = lax.broadcasted_iota(jnp.int32, (dims, 128), 0)
-    lengths = jnp.ones((dims, 128), F32)
-    for d in range(dims):
-        lengths = jnp.where(index == d, lengths_ref[d], lengths)
-    scale = ((KAPPA * math.sqrt(5.0)) / lengths)[:, :1]
-    scaled_ref[...] = points_ref[...] * scale
+def prepare_kernel(place_ref, points_ref, direction_ref, half_ref, low_ref):
+    half_ref[...] = points_ref[pl.ds(pl.multiple_of(place_ref[0] * 8, 8), 8), :]
     low_ref[...] = direction_ref[...].astype(BF16)
 
 
-def prepare(lengths, points, direction):
+def prepare(place, points, direction):
     vmem = pl.BlockSpec(memory_space=pltpu.VMEM)
     return pl.pallas_call(
         prepare_kernel,
         out_shape=(
-            jax.ShapeDtypeStruct(points.shape, F32),
+            jax.ShapeDtypeStruct((8, points.shape[1]), F32),
             jax.ShapeDtypeStruct(direction.shape, BF16),
         ),
         in_specs=[pl.BlockSpec(memory_space=pltpu.SMEM), vmem, vmem],
         out_specs=(vmem, vmem),
         compiler_params=pltpu.CompilerParams(vmem_limit_bytes=8 * 2**20),
         name="prepare",
-    )(lengths, points, direction)
-
-
-def pack_kernel(far, place_ref, scaled_ref, low_ref, other_ref, packets_ref):
-    yl, core = place_ref[0], place_ref[1]
+    )(place, points, direction)
+
+
+def pack_kernel(far, place_ref, half_ref, low_ref, other_ref, packets_ref):
+    core = place_ref[1]
     piece = low_ref.shape[1] // 4
     for q in range(2):
         here = pl.ds(pl.multiple_of((2 * q + core) * piece, piece), piece)
-        half = scaled_ref[pl.ds(pl.multiple_of(yl * 8, 8), 8), here]
-        parts = [low_ref[:, here], other_ref[:, here].astype(BF16), half.astype(BF16)]
+        parts = [low_ref[:, here], other_ref[:, here].astype(BF16), half_ref[:, here].astype(BF16)]
         packet = jnp.concatenate(parts, axis=1)
         for n in range(far):
             packets_ref[q * far + n] = packet
 
 
-def pack(far, place, scaled, low, other):
+def pack(far, place, half, low, other):
     vmem = pl.BlockSpec(memory_space=pltpu.VMEM)
     own, count = low.shape
     return pl.pallas_call(
@@ -267,7 +262,7 @@
         out_specs=vmem,
         compiler_params=pltpu.CompilerParams(vmem_limit_bytes=8 * 2**20),
         name="pack",
-    )(place, scaled, low, other)
+    )(place, half, low, other)
 
 
 def sums_kernel(scale_ref, noise_ref, direction_ref, residual_ref, solution_ref, *refs):
@@ -308,22 +303,24 @@
 
     place = jnp.stack([lax.axis_index("yl"), lax.axis_index("core")])
     other = lax.ppermute(direction, "core", swap)
-    scaled, low = prepare(lengths, points, direction)
-    packets = pack(far, place, scaled, low, other)
+    half, low = prepare(place, points, direction)
+    packets = pack(far, place, half, low, other)
     packets = lax.all_to_all(packets, ("yl", *FAR), 0, 0, tiled=True)
-    blocks = [scaled] + [
-        lax.ppermute(scaled, "x", [(i, i ^ step) for i in range(line)])
+    blocks = [points] + [
+        lax.ppermute(points, "x", [(i, i ^ step) for i in range(line)])
         for step in range(1, line)
     ]
-    rows = row_features(blocks)
+    factor = (KAPPA * math.sqrt(5.0)) / lengths
+    scale = jnp.broadcast_to(factor[:, None], (lengths.shape[0], 128))
+    rows = row_features(scale, blocks)
 
     def send(value, step):
         return lax.ppermute(value, "x", [(i, i ^ step) for i in range(line)])
 
-    packets, *rows = lax.optimization_barrier((packets, *rows))
-    near = col_features(place, packets)
+    packets, scale, *rows = lax.optimization_barrier((packets, scale, *rows))
+    near = col_features(place, scale, packets)
     others = kernel_image((rows[3], rows[2], rows[1]), (near,))
-    distant = col_features(place, lax.ppermute(packets, "yh", swap))
+    distant = col_features(place, scale, lax.ppermute(packets, "yh", swap))
     image3, image2, image1 = kernel_image((rows[3], rows[2], rows[1]), (distant,), others)
     image3, image2, image1 = send(image3, 3), send(image2, 2), send(image1, 1)
     (image0,) = kernel_image((rows[0],), (near, distant))

time: 83.3 us -> 83.2 us (level)
  waiting for transfers between devices: 7.86 us -> 8.72 us
    unnamed x14 -> x16, local copies, waits for them, and re-layouts: 2.19 us -> 1.62 us
  transfers between devices with their start and end apart: 11 -> 11, of which waited for: 4 -> 5; matrix products, arithmetic and copies ran while one was open for 0% -> 0% of each run, Pallas kernels for 20% -> 20%
where the time goes in v6:
time: 83.2 us; the launch traced here: 82.8 us
  Pallas kernels  27.3 us (33%)
  starting transfers between devices  22.5 us (27%)
  blocking collectives  20.2 us (24%)
  waiting for transfers between devices  8.72 us (10%)
  local copies, waits for them, and re-layouts  1.69 us (2%)
  between operations  1.44 us (2%)
  other arithmetic  0.96 us (1%)
    pallas_call x3, Pallas kernels, kernel_image(): pl.pallas_call(functools.partial(image_kernel, groups, sets, tile_i, tile...  23.4 us
    all_to_all x1, blocking collectives, local(): sums = lax.all_to_all(sums, BLK, 0, 0, tiled=True)  20.2 us
    all_to_all x1, starting transfers between devices, local(): packets = lax.all_to_all(packets, ('yl', *FAR), 0, 0, tiled=True)  10.1 us
    ppermute x3, waiting for transfers between devices, local(): lax.ppermute(points, 'x', [(i, i ^ step) for i in range(line)])  4.92 us
    ppermute x3, starting transfers between devices, send(): return lax.ppermute(value, 'x', [(i, i ^ step) for i in range(line)])  4.79 us
    ppermute x3, starting transfers between devices, local(): lax.ppermute(points, 'x', [(i, i ^ step) for i in range(line)])  4.25 us
    ppermute x1, waiting for transfers between devices, local(): parts = [keep, lax.ppermute(rest, 'yl', swap)]  2.55 us
    ppermute x1, starting transfers between devices, local(): distant = col_features(place, scale, lax.ppermute(packets, 'yh', swap))  2.38 us
  transfers between devices with their start and end apart: 11, of which 5 were waited for; matrix products, arithmetic and copies ran while one was open for 0% of the time, Pallas kernels for 20%

profile of v6, /device:TPU:8, one launch (start us, length us, event | category | flops | bytes accessed | tf_op | source)
XLA Modules:
  0.0 82.8 jit_solution(16484278191466584886)
XLA Ops:
  0.6 0.1 collective-permute-start
  0.7 0.1 pad_add_fusion.place_ref
  0.8 0.0 copy-start
  0.8 0.8 copy-done
  1.6 0.0 copy-start.2
  1.6 0.8 %copy-done.2 = f32[16,1024]{1,0:T(8,128)S(1)} copy-done((f32[16,1024]{1,0:T(8,128)S(1)}, f32[16,1024]{1,0:T(8,128)}, u32[]{:S(2)}) %copy-start.2) | copy-done | bytes 65560
  2.4 0.5 prepare.1
  3.0 0.0 collective-permute-done.other_ref
  3.0 1.3 %pack.1 = bf16[16,8,768]{2,1,0:T(8,128)(2,1)} custom-call(s32[2]{0:T(128)S(1)} %pad_add_fusion.place_ref, f32[8,1024]{1,0:T(8,128)S(1)} %get-tuple-element.32.half_ref, bf16[8,1024]{1,0:T(8,128)(2,1)S(1)} %get-tuple-element.33.low_ref, f32[8,1024]{1,0:T(8,128)S(1)} %collective-permute-done.other_ref), custom_call_target="tpu_custom_call" | custom-call | tf_op jit(solution)/shard_map/pack/pallas_call | solution.py:258
  4.2 0.0 copy-start.3
  4.2 0.0 copy-start.7
  4.2 10.1 %all-to-all-start = ((bf16[16,8,768]{2,1,0:T(8,128)(2,1)}), bf16[16,8,768]{2,1,0:T(8,128)(2,1)S(1)}, u32[]{:S(2)}, u32[]{:S(2)}) async-start(bf16[16,8,768]{2,1,0:T(8,128)(2,1)} %pack.1), calls=%async_computation | async-start | bytes 393216 | tf_op jit(solution)/shard_map/all_to_all | solution.py:308
  14.3 0.0 copy-done.3
  14.3 3.1 %collective-permute-start.2 = (f32[16,1024]{1,0:T(8,128)S(1)}, f32[16,1024]{1,0:T(8,128)S(1)}, u32[]{:S(2)}, u32[]{:S(2)}) collective-permute-start(f32[16,1024]{1,0:T(8,128)S(1)} %copy-done.3), channel_id=1, source_target_pairs={{0,8},{4,12},{8,0},{12,4},{1,9},{5,13},{9,1},{13,5},{2,10},{6,14},... | collective-permute-start | bytes 196616 | tf_op jit(solution)/shard_map/ppermute | solution.py:310
  17.4 0.6 collective-permute-start.1
  18.0 0.6 collective-permute-start.3
  18.6 0.0 copy-done.7
  18.6 1.6 %collective-permute-done.2.refs_2_ = f32[16,1024]{1,0:T(8,128)S(1)} collective-permute-done((f32[16,1024]{1,0:T(8,128)S(1)}, f32[16,1024]{1,0:T(8,128)S(1)}, u32[]{:S(2)}, u32[]{:S(2)}) %collective-permute-start.2) | collective-permute-done | bytes 65568 | tf_op jit(solution)/shard_map/ppermute | solution.py:310
  20.2 1.5 %collective-permute-done.1.refs_1_ = f32[16,1024]{1,0:T(8,128)S(1)} collective-permute-done((f32[16,1024]{1,0:T(8,128)S(1)}, f32[16,1024]{1,0:T(8,128)S(1)}, u32[]{:S(2)}, u32[]{:S(2)}) %collective-permute-start.1) | collective-permute-done | bytes 65568 | tf_op jit(solution)/shard_map/ppermute | solution.py:310
  21.7 1.8 %collective-permute-done.3.refs_3_ = f32[16,1024]{1,0:T(8,128)S(1)} collective-permute-done((f32[16,1024]{1,0:T(8,128)S(1)}, f32[16,1024]{1,0:T(8,128)S(1)}, u32[]{:S(2)}, u32[]{:S(2)}) %collective-permute-start.3) | collective-permute-done | bytes 65568 | tf_op jit(solution)/shard_map/ppermute | solution.py:310
  23.5 0.1 broadcast_in_dim.5.scale_ref
  23.6 0.2 row_features.1
  23.8 0.0 all-to-all-done.packets_ref
  23.8 2.4 %collective-permute-start.4 = (bf16[16,8,768]{2,1,0:T(8,128)(2,1)S(1)}, bf16[16,8,768]{2,1,0:T(8,128)(2,1)S(1)}, u32[]{:S(2)}, u32[]{:S(2)}) collective-permute-start(bf16[16,8,768]{2,1,0:T(8,128)(2,1)S(1)} %all-to-all-done.packets_ref), channel_id=1, source_target_pairs={{0,16},{16,0},{1,17},{17,1},{2,18},{18,2},{3,19},{19,3},{4,20},{20... | collective-permute-start | bytes 589832 | tf_op jit(solution)/shard_map/ppermute | solution.py:323
  26.2 0.9 %col_features.2 = (bf16[2048,64]{1,0:T(8,128)(2,1)S(1)}, bf16[32,2048]{1,0:T(8,128)(2,1)S(1)}) custom-call(s32[2]{0:T(128)S(1)} %pad_add_fusion.place_ref, f32[16,128]{1,0:T(8,128)S(1)} %broadcast_in_dim.5.scale_ref, bf16[16,8,768]{2,1,0:T(8,128)(2,1)S(1)} %all-to-all-done.packets_ref), custom_call_target="tpu_custom_call" | custom-call | tf_op jit(solution)/shard_map/col_features/pallas_call | solution.py:88
  27.1 8.7 %kernel_image.4 = (f32[32,1024]{1,0:T(8,128)S(1)}, f32[32,1024]{1,0:T(8,128)S(1)}, f32[32,1024]{1,0:T(8,128)S(1)}) custom-call(bf16[64,1024]{1,0:T(8,128)(2,1)S(1)} %get-tuple-element.45.refs_0_, bf16[64,1024]{1,0:T(8,128)(2,1)S(1)} %get-tuple-element.46.refs_1_, bf16[64,1024]{1,0:T(8,128)(2,1)S(1)} %get-tuple-element.47.refs_2_, ...), custom_call_target="tpu_custom_call" | custom-call | flops 1207959552 | bytes 4194304 | tf_op jit(solution)/shard_map/kernel_image/pallas_call | solution.py:178
  35.8 0.0 collective-permute-done.4.packets_ref
  35.8 0.9 %col_features.3 = (bf16[2048,64]{1,0:T(8,128)(2,1)S(1)}, bf16[32,2048]{1,0:T(8,128)(2,1)S(1)}) custom-call(s32[2]{0:T(128)S(1)} %pad_add_fusion.place_ref, f32[16,128]{1,0:T(8,128)S(1)} %broadcast_in_dim.5.scale_ref, bf16[16,8,768]{2,1,0:T(8,128)(2,1)S(1)} %collective-permute-done.4.packets_ref), custom_call_target="tpu_custom_call" | custom-call | tf_op jit(solution)/shard_map/col_features/pallas_call | solution.py:88
  36.6 8.7 %kernel_image.5 = (f32[32,1024]{1,0:T(8,128)S(1)}, f32[32,1024]{1,0:T(8,128)S(1)}, f32[32,1024]{1,0:T(8,128)S(1)}) custom-call(bf16[64,1024]{1,0:T(8,128)(2,1)S(1)} %get-tuple-element.45.refs_0_, bf16[64,1024]{1,0:T(8,128)(2,1)S(1)} %get-tuple-element.46.refs_1_, bf16[64,1024]{1,0:T(8,128)(2,1)S(1)} %get-tuple-element.47.refs_2_, ...), custom_call_target="tpu_custom_call" | custom-call | flops 1207959552 | bytes 4194304 | tf_op jit(solution)/shard_map/kernel_image/pallas_call | solution.py:178
  45.3 0.5 collective-permute-start.5
  45.8 2.7 %collective-permute-start.6 = (f32[32,1024]{1,0:T(8,128)S(1)}, f32[32,1024]{1,0:T(8,128)S(1)}, u32[]{:S(2)}, u32[]{:S(2)}) collective-permute-start(f32[32,1024]{1,0:T(8,128)S(1)} %get-tuple-element.52), channel_id=1, source_target_pairs={{0,8},{4,12},{8,0},{12,4},{1,9},{5,13},{9,1},{13,5},{2,10},{6,14},... | collective-permute-start | bytes 393224 | tf_op jit(solution)/shard_map/ppermute | solution.py:318
  48.5 1.6 %collective-permute-start.7 = (f32[32,1024]{1,0:T(8,128)S(1)}, f32[32,1024]{1,0:T(8,128)S(1)}, u32[]{:S(2)}, u32[]{:S(2)}) collective-permute-start(f32[32,1024]{1,0:T(8,128)S(1)} %get-tuple-element.53), channel_id=1, source_target_pairs={{0,12},{4,8},{8,4},{12,0},{1,13},{5,9},{9,5},{13,1},{2,14},{6,10},... | collective-permute-start | bytes 393224 | tf_op jit(solution)/shard_map/ppermute | solution.py:318
  50.1 6.1 %kernel_image.3.refs_0_ = f32[32,1024]{1,0:T(8,128)S(1)} custom-call(bf16[64,1024]{1,0:T(8,128)(2,1)S(1)} %get-tuple-element.38.refs_0_, bf16[2048,64]{1,0:T(8,128)(2,1)S(1)} %get-tuple-element.41.refs_1_.refs_3_, bf16[2048,64]{1,0:T(8,128)(2,1)S(1)} %get-tuple-element.42.refs_2_.refs_3_, bf16[32,2048]{1,0:T(8,128)(2,1)S(1)} %get-tuple-element.43.refs_3_.refs_4_, ...), custom_call_target="tpu_custom_call" | custom-call | flops 805306368 | bytes 4194304 | tf_op jit(solution)/shard_map/kernel_image/pallas_call | solution.py:178
  56.2 0.0 collective-permute-done.5.refs_1_
  56.2 0.0 collective-permute-done.6.refs_2_
  56.2 0.0 collective-permute-done.7.refs_3_
  56.2 0.1 collective-permute-start.8
  56.3 1.2 %collective-permute-done.8.refs_1_ = f32[16,1024]{1,0:T(8,128)S(1)} collective-permute-done((f32[16,1024]{1,0:T(8,128)S(1)}, f32[16,1024]{1,0:T(8,128)S(1)}, u32[]{:S(2)}, u32[]{:S(2)}) %collective-permute-start.8) | collective-permute-done | bytes 65568 | tf_op jit(solution)/shard_map/ppermute | solution.py:328
  57.6 0.0 copy-start.1
  57.6 0.0 copy-start.4
  57.6 0.0 copy-start.5
  57.6 0.0 copy-start.6
  57.6 0.8 collective-permute-start.9
  59.1 2.5 %collective-permute-done.9.refs_1_ = f32[8,1024]{1,0:T(8,128)S(1)} collective-permute-done((f32[8,1024]{1,0:T(8,128)S(1)}, f32[8,1024]{1,0:T(8,128)S(1)}, u32[]{:S(2)}, u32[]{:S(2)}) %collective-permute-start.9) | collective-permute-done | bytes 32800 | tf_op jit(solution)/shard_map/ppermute | solution.py:329
  61.6 0.0 copy-done.1
  61.6 0.0 copy-done.4
  61.6 0.0 copy-done.5
  61.6 0.0 copy-done.6
  61.6 0.1 column_sums.1
  61.7 20.2 %all_to_all.14 = f32[64,1,128]{2,1,0:T(1,128)S(1)} all-to-all(f32[64,1,128]{2,1,0:T(1,128)S(1)} %bitcast.6), channel_id=1, replica_groups=mesh['z'=8,'yh'=2,'x'=4,'yl'=2,'core'=2] {'z','yh','x'}, dimensions={0} | all-to-all | bytes 65536 | tf_op jit(solution)/shard_map/all_to_all | solution.py:333
  81.9 0.1 reduce_sum.9
  82.0 0.1 maximum_divide_fusion
  82.1 0.7 multiply_add_fusion
  (3 shorter events, 0.0 us)
Async XLA Ops:
  0.6 2.3 %collective-permute-start = (f32[8,1024]{1,0:T(8,128)}, f32[8,1024]{1,0:T(8,128)S(1)}, u32[]{:S(2)}, u32[]{:S(2)}) collective-permute-start(f32[8,1024]{1,0:T(8,128)} %direction_ref.3), channel_id=1, source_target_pairs={{0,1},{1,0},{2,3},{3,2},{4,5},{5,4},{6,7},{7,6},{8,9},{9,8},{10,11... | collective-permute-start | bytes 98312 | tf_op jit(solution)/shard_map/ppermute | solution.py:305
  0.8 0.8 copy-start
  1.6 0.8 %copy-start.2 = (f32[16,1024]{1,0:T(8,128)S(1)}, f32[16,1024]{1,0:T(8,128)}, u32[]{:S(2)}) copy-start(f32[16,1024]{1,0:T(8,128)} %refs_0_.1) | copy-start | bytes 196612
  4.2 10.1 %copy-start.3 = (f32[16,1024]{1,0:T(8,128)S(1)}, f32[16,1024]{1,0:T(8,128)}, u32[]{:S(2)}) copy-start(f32[16,1024]{1,0:T(8,128)} %refs_0_.1) | copy-start | bytes 196612
  4.2 14.3 %copy-start.7 = (f32[16]{0:T(128)S(1)}, f32[16]{0:T(128)}, u32[]{:S(2)}) copy-start(f32[16]{0:T(128)} %param.8) | copy-start | bytes 196
  4.2 19.6 %all-to-all-start = ((bf16[16,8,768]{2,1,0:T(8,128)(2,1)}), bf16[16,8,768]{2,1,0:T(8,128)(2,1)S(1)}, u32[]{:S(2)}, u32[]{:S(2)}) async-start(bf16[16,8,768]{2,1,0:T(8,128)(2,1)} %pack.1), calls=%async_computation | async-start | bytes 393216 | tf_op jit(solution)/shard_map/all_to_all | solution.py:308
  14.3 5.9 %collective-permute-start.2 = (f32[16,1024]{1,0:T(8,128)S(1)}, f32[16,1024]{1,0:T(8,128)S(1)}, u32[]{:S(2)}, u32[]{:S(2)}) collective-permute-start(f32[16,1024]{1,0:T(8,128)S(1)} %copy-done.3), channel_id=1, source_target_pairs={{0,8},{4,12},{8,0},{12,4},{1,9},{5,13},{9,1},{13,5},{2,10},{6,14},... | collective-permute-start | bytes 196616 | tf_op jit(solution)/shard_map/ppermute | solution.py:310
  17.4 4.3 %collective-permute-start.1 = (f32[16,1024]{1,0:T(8,128)S(1)}, f32[16,1024]{1,0:T(8,128)S(1)}, u32[]{:S(2)}, u32[]{:S(2)}) collective-permute-start(f32[16,1024]{1,0:T(8,128)S(1)} %copy-done.3), channel_id=1, source_target_pairs={{0,4},{4,0},{8,12},{12,8},{1,5},{5,1},{9,13},{13,9},{2,6},{6,2},{1... | collective-permute-start | bytes 196616 | tf_op jit(solution)/shard_map/ppermute | solution.py:310
  18.0 5.5 %collective-permute-start.3 = (f32[16,1024]{1,0:T(8,128)S(1)}, f32[16,1024]{1,0:T(8,128)S(1)}, u32[]{:S(2)}, u32[]{:S(2)}) collective-permute-start(f32[16,1024]{1,0:T(8,128)S(1)} %copy-done.3), channel_id=1, source_target_pairs={{0,12},{4,8},{8,4},{12,0},{1,13},{5,9},{9,5},{13,1},{2,14},{6,10},... | collective-permute-start | bytes 196616 | tf_op jit(solution)/shard_map/ppermute | solution.py:310
  23.8 11.9 %collective-permute-start.4 = (bf16[16,8,768]{2,1,0:T(8,128)(2,1)S(1)}, bf16[16,8,768]{2,1,0:T(8,128)(2,1)S(1)}, u32[]{:S(2)}, u32[]{:S(2)}) collective-permute-start(bf16[16,8,768]{2,1,0:T(8,128)(2,1)S(1)} %all-to-all-done.packets_ref), channel_id=1, source_target_pairs={{0,16},{16,0},{1,17},{17,1},{2,18},{18,2},{3,19},{19,3},{4,20},{20... | collective-permute-start | bytes 589832 | tf_op jit(solution)/shard_map/ppermute | solution.py:323
  45.3 10.9 %collective-permute-start.5 = (f32[32,1024]{1,0:T(8,128)S(1)}, f32[32,1024]{1,0:T(8,128)S(1)}, u32[]{:S(2)}, u32[]{:S(2)}) collective-permute-start(f32[32,1024]{1,0:T(8,128)S(1)} %get-tuple-element.51), channel_id=1, source_target_pairs={{0,4},{4,0},{8,12},{12,8},{1,5},{5,1},{9,13},{13,9},{2,6},{6,2},{1... | collective-permute-start | bytes 393224 | tf_op jit(solution)/shard_map/ppermute | solution.py:318
  45.8 10.4 %collective-permute-start.6 = (f32[32,1024]{1,0:T(8,128)S(1)}, f32[32,1024]{1,0:T(8,128)S(1)}, u32[]{:S(2)}, u32[]{:S(2)}) collective-permute-start(f32[32,1024]{1,0:T(8,128)S(1)} %get-tuple-element.52), channel_id=1, source_target_pairs={{0,8},{4,12},{8,0},{12,4},{1,9},{5,13},{9,1},{13,5},{2,10},{6,14},... | collective-permute-start | bytes 393224 | tf_op jit(solution)/shard_map/ppermute | solution.py:318
  48.5 7.7 %collective-permute-start.7 = (f32[32,1024]{1,0:T(8,128)S(1)}, f32[32,1024]{1,0:T(8,128)S(1)}, u32[]{:S(2)}, u32[]{:S(2)}) collective-permute-start(f32[32,1024]{1,0:T(8,128)S(1)} %get-tuple-element.53), channel_id=1, source_target_pairs={{0,12},{4,8},{8,4},{12,0},{1,13},{5,9},{9,5},{13,1},{2,14},{6,10},... | collective-permute-start | bytes 393224 | tf_op jit(solution)/shard_map/ppermute | solution.py:318
  56.2 1.3 %collective-permute-start.8 = (f32[16,1024]{1,0:T(8,128)S(1)}, f32[16,1024]{1,0:T(8,128)S(1)}, u32[]{:S(2)}, u32[]{:S(2)}) collective-permute-start(f32[16,1024]{1,0:T(8,128)S(1)} %get-tuple-element.55), channel_id=1, source_target_pairs={{0,1},{1,0},{2,3},{3,2},{4,5},{5,4},{6,7},{7,6},{8,9},{9,8},{10,11... | collective-permute-start | bytes 196616 | tf_op jit(solution)/shard_map/ppermute | solution.py:328
  57.6 4.0 %copy-start.1 = (f32[8,1024]{1,0:T(8,128)S(1)}, f32[8,1024]{1,0:T(8,128)}, u32[]{:S(2)}) copy-start(f32[8,1024]{1,0:T(8,128)} %direction_ref.3) | copy-start | bytes 98308
  57.6 4.0 %copy-start.4 = (f32[8,1024]{1,0:T(8,128)S(1)}, f32[8,1024]{1,0:T(8,128)}, u32[]{:S(2)}) copy-start(f32[8,1024]{1,0:T(8,128)} %residual_ref.1) | copy-start | bytes 98308
  57.6 4.0 %copy-start.5 = (f32[8,1024]{1,0:T(8,128)S(1)}, f32[8,1024]{1,0:T(8,128)}, u32[]{:S(2)}) copy-start(f32[8,1024]{1,0:T(8,128)} %solution_ref.1) | copy-start | bytes 98308
  57.6 4.0 %copy-start.6 = (f32[1024]{0:T(1024)S(1)}, f32[1024]{0:T(1024)}, u32[]{:S(2)}) copy-start(f32[1024]{0:T(1024)} %param.9) | copy-start | bytes 12292
  57.6 4.0 %collective-permute-start.9 = (f32[8,1024]{1,0:T(8,128)S(1)}, f32[8,1024]{1,0:T(8,128)S(1)}, u32[]{:S(2)}, u32[]{:S(2)}) collective-permute-start(f32[8,1024]{1,0:T(8,128)S(1)} %get-tuple-element.57), channel_id=1, source_target_pairs={{0,2},{2,0},{1,3},{3,1},{4,6},{6,4},{5,7},{7,5},{8,10},{10,8},{9,1... | collective-permute-start | bytes 98312 | tf_op jit(solution)/shard_map/ppermute | solution.py:329
